TPU v7x, 32 devices: a whole 2x2x4 slice. The times are simulated.
32 devices in a mesh: depth: 4 (over y, x), tile: 8 (over z, core).
Axes of the slice: x: 2, y: 2, z: 4, core: 2. Of those that a mesh axis runs over, the one named last changes fastest.
Arguments:
- source: bfloat16 [16, 2, 128, 256], P('tile'), may hold values from -6 to 6
- anchors: int32 [16], P('tile'), may hold values from -256 to 1792, as said below
- counts: int32 [4], P('depth'), may hold values from 1 to 3, 8 in all
- reflect: bfloat16 [4, 3, 128, 2048], P('depth', None, None, 'tile'), may hold values from -0.3984375 to 0.3984375
- lateral_x: bfloat16 [4, 3, 2, 128, 128], P('depth'), may hold values from -0.375 to 0.375
- lateral_y: bfloat16 [4, 3, 2, 256, 256], P('depth'), may hold values from -0.25 to 0.25
Outputs:
- image: float32 [4, 3, 128, 2048], P('depth', None, None, 'tile')
Inputs may be any that keep to these rules, and one draw needn't show every extreme that they name: `anchors`: the shots held by tile index t start their aperture between (t - 1) * 256 and t * 256. The counts sum to 8; slots at or past a section's count are unused.
All inputs are finite; a program needn't handle non-finite values. No bound on the sum of `counts` on one device may be relied on, other than what follows from the above.
Results may differ from a plain program's by a relative error of at most 0.023.
Values may be sent and summed in bfloat16 or wider, within the bound.
No kernel may reach another device: no remote copies, remote signals or barrier semaphores. Data moves between devices by JAX's collectives and lax.ppermute only.
A program may use at most 64 MiB of HBM per device.

v0:
```python
import functools

import jax
import jax.numpy as jnp
from jax import lax
from jax.experimental import pallas as pl
from jax.experimental.pallas import tpu as pltpu
from jax.sharding import PartitionSpec as P

BOTH = ("depth", "tile")
MIB = 1024 * 1024
TAIL = 16


class Plan:
    def __init__(self, shots):
        self.sections = lax.axis_size("depth")
        self.tiles = lax.axis_size("tile")
        self.shots = shots
        self.group = self.sections // shots
        assert self.sections == 4 and self.group * shots == self.sections
        assert self.tiles % (2 * self.group) == 0

    def device(self, depth, tile):
        return depth * self.tiles + tile

    def bases(self):
        return range(0, self.tiles, self.group)

    def worker(self, base, w):
        return self.device(w, base + w // self.shots)

    def other(self, w, base):
        return self.device(w, base + (w // self.shots + 1) % self.group)

    def ops_to_workers(self, r):
        return [
            (self.other(w ^ r, base), self.worker(base, w))
            for base in self.bases()
            for w in range(self.sections)
        ]

    def swap_workers(self):
        return [
            (self.worker(base, w), self.worker((base // self.group ^ 1) * self.group, w))
            for base in self.bases()
            for w in range(self.sections)
        ]

    def to_workers(self, r):
        return [
            (self.device(w ^ r, base + w // self.shots), self.worker(base, w))
            for base in self.bases()
            for w in range(self.sections)
        ]

    def from_workers(self, r):
        return [(b, a) for a, b in self.to_workers(r)]


def pack_kernel(group, sizes, x_hbm, y_hbm, even, odd, late, half_out, x_ref, y_ref, sem):
    slots, rows, columns = sizes
    loads = [
        pltpu.make_async_copy(x_hbm, x_ref, sem.at[0]),
        pltpu.make_async_copy(y_hbm, y_ref, sem.at[1]),
    ]
    for load in loads:
        load.start()
    for load in loads:
        load.wait()
    piece = rows // 2
    part = columns + piece
    first = (slots - 1) * part
    for half in range(2):
        for slot in range(slots):
            op_x = jnp.concatenate(
                [x_ref[slot, i, half * piece : (half + 1) * piece, :] for i in range(2)], axis=1
            )
            op_y = y_ref[slot, half]
            if slot < slots - 1:
                places = [(out, half * first + slot * part) for out in (even, odd)]
            else:
                places = [(late, half * part)]
            for out, spot in places:
                out[spot : spot + columns, :] = op_y
                out[spot + columns : spot + part, :] = op_x
    plane = lax.rem(lax.axis_index("tile") // group, 2)
    half_out[:first, :] = even[pl.ds(pl.multiple_of(plane * first, first), first), :]
    half_out[first:, :] = late[pl.ds(pl.multiple_of(plane * part, part), part), :]


def window_kernel(shots, sizes, anchors_hbm, counts, left_ref, right_hbm, *refs):
    slots, rows, columns = sizes
    messages, (alone, anchors, right_ref, sem) = refs[shots : 2 * shots], refs[2 * shots :]
    loads = [
        pltpu.make_async_copy(anchors_hbm, anchors, sem.at[0]),
        pltpu.make_async_copy(right_hbm, right_ref, sem.at[1]),
    ]
    for load in loads:
        load.start()
    for load in loads:
        load.wait()
    section, tile = lax.axis_index("depth"), lax.axis_index("tile")
    left, right = left_ref[...].astype(jnp.float32), right_ref[...].astype(jnp.float32)
    lanes = lax.broadcasted_iota(jnp.int32, left.shape, 1)
    tail = jnp.full((TAIL, columns), counts[0].astype(jnp.float32), jnp.float32)
    for q, message in enumerate(messages):
        offset = anchors[lax.rem(section, shots) ^ q] - (tile - 1) * columns
        merged = jnp.where(lanes >= offset, left, right)
        back = lax.rem(columns - lax.rem(offset, columns), columns)
        window = pltpu.roll(merged, back, 1).astype(message.dtype)
        for out in [message] + ([alone] if q == shots - 1 else []):
            spot = out.shape[0] - TAIL - slots * rows
            out[spot : spot + slots * rows, :] = window
            out[spot + slots * rows :, :] = tail.astype(out.dtype)


class Sweep:
    def __init__(self, shots, group, sizes, turned_y, turned_x, level_w, waves, stage_y, stage_x):
        self.sizes = sizes
        self.turned_y, self.turned_x, self.level_w = turned_y, turned_x, level_w
        self.waves, self.stage_y, self.stage_x = waves, stage_y, stage_x
        slots, rows, columns = sizes
        self.piece = rows // 2
        self.part = columns + self.piece
        self.first = (slots - 1) * self.part
        self.half_rows = self.first + self.part
        self.win_rows = slots * rows + TAIL
        self.here, tile = lax.axis_index("depth"), lax.axis_index("tile")
        self.shot = lax.rem(self.here, shots)
        self.is_worker = (self.here // shots == lax.rem(tile, group)).astype(jnp.int32)

    def read_counts(self, sources, counts):
        for r, (_, _, window) in enumerate(sources):
            value = jnp.max(window[window.shape[0] - TAIL :, :].astype(jnp.float32))
            counts[r] = value.astype(jnp.int32)

    def early_slots(self, r, count, rounds):
        partial = (r != 0) & (r != rounds - 1)
        return jnp.where(partial, jnp.minimum(count, self.sizes[0] - 1), count)

    def window_start(self, window_ref):
        return window_ref.shape[0] - self.win_rows

    def fetch(self, r, slot, place, sources):
        slots, rows, columns = self.sizes
        for r_of, (early, late, window) in enumerate(sources):
            early_slots = slots if early.shape[0] == 2 * self.half_rows else slots - 1
            choices = [(early, early_slots * self.part, slot < early_slots, slot)]
            if late is not None:
                choices.append((late, self.part, slot == slots - 1, 0))
            for ref, stride, chosen, at in choices:

                @pl.when((r == r_of) & chosen)
                def _():
                    for half in range(2):
                        start = pl.multiple_of(half * stride + at * self.part, self.piece)
                        self.stage_y[half * columns : (half + 1) * columns, :] = ref[
                            pl.ds(start, columns), :
                        ]
                        tail = pl.multiple_of(start + columns, self.piece)
                        self.stage_x[half * self.piece : (half + 1) * self.piece, :] = ref[
                            pl.ds(tail, self.piece), :
                        ]
                    spot = self.window_start(window) + slot * rows
                    self.level_w[place] = window[pl.ds(pl.multiple_of(spot, TAIL), rows), :]

    def blocks(self, re, im):
        upper = jnp.concatenate([re, -im], axis=1)
        return jnp.concatenate([upper, jnp.concatenate([im, re], axis=1)], axis=0)

    def complex_sum(self, both):
        _, rows, columns = self.sizes
        with_re, with_im = both[:, :columns], both[:, columns:]
        return with_re[:rows] - with_im[rows:], with_im[:rows] + with_re[rows:]

    def dot(self, a, b, dims):
        return lax.dot_general(a, b, (dims, ((), ())), preferred_element_type=jnp.float32)

    def down(self, place):
        _, rows, columns = self.sizes
        x_re, x_im = self.stage_x[:, :rows], self.stage_x[:, rows:]
        wave = self.waves[place].astype(jnp.float32)
        gain = 1.0 + self.level_w[place].astype(jnp.float32)
        scaled = jnp.concatenate([gain * wave[:rows], gain * wave[rows:]], axis=0)
        self.turned_x[place] = self.blocks(x_re.T, x_im.T)
        middle = self.dot(self.blocks(x_re, x_im), scaled.astype(jnp.bfloat16), ((1,), (0,)))
        for i in range(2):
            lines = slice(i * columns, (i + 1) * columns)
            self.turned_y[place, lines, :] = self.stage_y[lines, :].T
        both = self.dot(middle.astype(jnp.bfloat16), self.stage_y[...], ((1,), (1,)))
        moved = jnp.concatenate(self.complex_sum(both), axis=0)
        self.waves[place + 1] = moved.astype(jnp.bfloat16)
        return place + 1

    def up(self, r, slot, place, wave_up, outs):
        _, rows, columns = self.sizes
        level = place - 1
        wave = self.waves[level].astype(jnp.float32)
        window = self.level_w[level].astype(jnp.float32)
        back = self.dot(self.turned_x[level], wave_up[...], ((1,), (0,)))
        both = self.dot(back.astype(jnp.bfloat16), self.turned_y[level], ((1,), (1,)))
        spread_re, spread_im = self.complex_sum(both)
        up_re = (window * wave[:rows] + spread_re).astype(jnp.bfloat16)
        up_im = (window * wave[rows:] + spread_im).astype(jnp.bfloat16)
        wave_up[:rows] = up_re
        wave_up[rows:] = up_im
        product = wave[:rows] * up_re.astype(jnp.float32)
        product += wave[rows:] * up_im.astype(jnp.float32)
        spot = pl.multiple_of(slot * rows, rows)
        for r_of, out in enumerate(outs):

            @pl.when(r == r_of)
            def _():
                out[pl.ds(spot, rows), :] = product.astype(out.dtype)

        return level


def down_kernel(sections, shots, group, sizes, source_ref, *refs):
    (own, near, far), (own_late, joined, far_window) = refs[:3], refs[3:6]
    *buffers, stage_y, stage_x, counts = refs[6:]
    it = Sweep(shots, group, sizes, *buffers, stage_y, stage_x)
    sources = [
        (own, own_late, own),
        (near, None, near),
        (far, None, far),
        (joined, None, far_window),
    ]

    @pl.when(it.is_worker != 0)
    def _():
        it.waves[0] = source_ref[it.shot]
        it.read_counts(sources, counts)

        def section_down(section, carry):
            place, going = carry
            r = section ^ it.here
            ready = it.early_slots(r, counts[r], sections)

            def level_down(slot, place):
                it.fetch(r, slot, place, sources)
                return it.down(place)

            place = lax.fori_loop(0, jnp.where(going, ready, 0), level_down, place)
            return place, going & (ready == counts[r])

        lax.fori_loop(0, sections, section_down, (jnp.int32(0), jnp.bool_(True)))


def up_kernel(sections, shots, group, sizes, *refs):
    (own, near, far), (own_late, near_late, far_late, joined, far_window) = refs[:3], refs[3:8]
    outs, refs = refs[12 : 12 + sections], refs[12 + sections :]
    *buffers, stage_y, stage_x, wave_up, counts = refs
    it = Sweep(shots, group, sizes, *buffers, stage_y, stage_x)
    sources = [
        (own, own_late, own),
        (near, near_late, near),
        (far, far_late, far),
        (joined, None, far_window),
    ]

    @pl.when(it.is_worker == 0)
    def _():
        outs[0][...] = jnp.zeros(outs[0].shape, outs[0].dtype)

    @pl.when(it.is_worker != 0)
    def _():
        it.read_counts(sources, counts)
        for out in outs:
            out[...] = jnp.zeros(out.shape, out.dtype)
        wave_up[...] = jnp.zeros(wave_up.shape, wave_up.dtype)

        def section_down(section, carry):
            place, going = carry
            r = section ^ it.here
            done = jnp.where(going, it.early_slots(r, counts[r], sections), 0)

            def level_down(slot, place):
                it.fetch(r, slot, place, sources)
                return it.down(place)

            place = lax.fori_loop(done, counts[r], level_down, place + done)
            return place, going & (done == counts[r])

        last, _ = lax.fori_loop(0, sections, section_down, (jnp.int32(0), jnp.bool_(True)))

        def section_up(step, place):
            r = (sections - 1 - step) ^ it.here
            count = counts[r]
            return lax.fori_loop(
                0,
                count,
                lambda inner, place: it.up(r, count - 1 - inner, place, wave_up, outs),
                place,
            )

        lax.fori_loop(0, sections, section_up, last)


def join_kernel(shots, group, anchors, first_ref, second_ref, out_ref, shifts):
    section, tile = lax.axis_index("depth"), lax.axis_index("tile")
    plane = lax.rem(tile // group, 2)
    half_rows = first_ref.shape[0]
    for i, ref in enumerate((first_ref, second_ref)):
        start = pl.multiple_of((plane if i == 0 else 1 - plane) * half_rows, half_rows)
        out_ref[pl.ds(start, half_rows), :] = ref[...]
    columns = shifts.shape[1]
    place = lax.broadcasted_iota(jnp.int32, shifts.shape[1:], 1)
    start = lax.broadcasted_iota(jnp.int32, shifts.shape[1:], 0)
    for q in range(shots):
        offset = anchors[lax.rem(section, shots) ^ q] - (tile - 1) * columns
        shifts[q] = (place - start == offset).astype(jnp.float32).astype(shifts.dtype)


def hold_kernel(array_ref, after_ref, out_ref):
    pass


def place_kernel(shots, shifts, *refs):
    arrived, (left_out, own_out) = refs[:-2], refs[-2:]
    places, columns = left_out.shape
    placed = None
    for q in range(shots):
        total = None
        for r in range(q, len(arrived), shots):
            value = arrived[r][:places, :]
            total = value if total is None else total + value
        part = jnp.dot(total, shifts[q], preferred_element_type=jnp.float32)
        placed = part if placed is None else placed + part
    left_out[...] = placed[:, :columns].astype(left_out.dtype)
    own_out[...] = placed[:, columns:]


def kept(array):
    return pltpu.with_memory_space_constraint(array, pltpu.HBM)


def held(array):
    return pltpu.with_memory_space_constraint(array, pltpu.VMEM)


def on_device(source, anchors, counts, reflect, lateral_x, lateral_y):
    shots, _, rows, columns = source.shape
    slots = reflect.shape[1]
    sizes = (slots, rows, columns)
    plan = Plan(shots)
    sections, group = plan.sections, plan.group
    assert shots == 2
    bf16 = jnp.bfloat16
    smem = pl.BlockSpec(memory_space=pltpu.SMEM)
    vmem = pl.BlockSpec(memory_space=pltpu.VMEM)
    hbm = pl.BlockSpec(memory_space=pltpu.HBM)
    anywhere = pl.BlockSpec(memory_space=pl.ANY)

    def params(mib):
        return pltpu.CompilerParams(vmem_limit_bytes=mib * MIB)

    tile_reflect = reflect[0].reshape(slots * rows, columns)
    halo = lax.ppermute(tile_reflect, "tile", [(i, i + 1) for i in range(plan.tiles - 1)])
    part = columns + rows // 2
    half_rows, win_rows = slots * part, slots * rows + TAIL
    early_rows = 2 * (half_rows - part) + win_rows
    even = pltpu.VMEM((early_rows + 5 * TAIL, columns), bf16)
    odd = pltpu.VMEM((early_rows, columns), bf16)
    even_early, odd_early, late, far_half = pl.pallas_call(
        functools.partial(pack_kernel, group, sizes),
        out_shape=[
            even,
            odd,
            jax.ShapeDtypeStruct((2 * part, columns), bf16),
            jax.ShapeDtypeStruct((half_rows, columns), bf16),
        ],
        in_specs=[hbm, hbm],
        out_specs=[vmem] * 4,
        scratch_shapes=[
            pltpu.VMEM(lateral_x.shape[1:], bf16),
            pltpu.VMEM(lateral_y.shape[1:], bf16),
            pltpu.SemaphoreType.DMA((2,)),
        ],
        compiler_params=params(12),
        name="pack",
    )(kept(lateral_x[0]), kept(lateral_y[0]))
    last = sections - 1
    far_half = lax.ppermute(far_half, BOTH, plan.to_workers(last))
    even_early, odd_early, far_window = pl.pallas_call(
        functools.partial(window_kernel, shots, sizes),
        out_shape=[even, odd, jax.ShapeDtypeStruct((win_rows, columns), bf16)],
        in_specs=[hbm, smem, vmem, hbm, vmem, vmem],
        out_specs=[vmem] * 3,
        scratch_shapes=[
            pltpu.SMEM((shots,), jnp.int32),
            pltpu.VMEM((slots * rows, columns), bf16),
            pltpu.SemaphoreType.DMA((2,)),
        ],
        input_output_aliases={4: 0, 5: 1},
        compiler_params=params(12),
        cost_estimate=pl.CostEstimate(flops=3 * 10**9, bytes_accessed=4 * MIB, transcendentals=0),
        name="windows",
    )(kept(anchors), counts, halo, kept(tile_reflect), held(even_early), held(odd_early))
    messages = [
        even_early,
        lax.ppermute(odd_early, BOTH, plan.to_workers(1)),
        lax.ppermute(even_early, BOTH, plan.to_workers(2)),
    ]
    far_window = lax.ppermute(far_window, BOTH, plan.to_workers(last))
    other_half = lax.ppermute(far_half, BOTH, plan.swap_workers())
    late = pl.pallas_call(
        hold_kernel,
        out_shape=jax.ShapeDtypeStruct(late.shape, bf16),
        in_specs=[anywhere] * 2,
        out_specs=anywhere,
        input_output_aliases={0: 0},
        compiler_params=params(2),
        cost_estimate=pl.CostEstimate(flops=36 * 10**8, bytes_accessed=0, transcendentals=0),
        name="hold",
    )(late, far_window)
    lates = [lax.ppermute(late, BOTH, plan.ops_to_workers(r)) for r in (1, 2)]
    joined, shifts = pl.pallas_call(
        functools.partial(join_kernel, shots, group),
        out_shape=[
            pltpu.VMEM((2 * half_rows, columns), bf16),
            pltpu.VMEM((shots, columns, 2 * columns), bf16),
        ],
        in_specs=[smem] + [vmem] * 2,
        out_specs=[vmem] * 2,
        compiler_params=params(8),
        name="join",
    )(anchors, held(far_half), held(other_half))

    levels = sections * slots
    buffers = [
        pltpu.VMEM((levels, 2 * columns, columns), bf16),
        pltpu.VMEM((levels, 2 * rows, 2 * rows), bf16),
        pltpu.VMEM((levels, rows, columns), bf16),
        pltpu.VMEM((levels + 1, 2 * rows, columns), bf16),
    ]
    stages = [pltpu.VMEM((2 * columns, columns), bf16), pltpu.VMEM((rows, 2 * rows), bf16)]
    messages = [held(message) for message in messages]
    late, joined, far_window = held(late), held(joined), held(far_window)
    filled = pl.pallas_call(
        functools.partial(down_kernel, sections, shots, group, sizes),
        out_shape=buffers,
        in_specs=[vmem] * 7,
        out_specs=[vmem] * 4,
        scratch_shapes=stages + [pltpu.SMEM((sections,), jnp.int32)],
        compiler_params=params(24),
        name="down",
    )(held(source.reshape(shots, 2 * rows, columns)), *messages, late, joined, far_window)
    correlations = pl.pallas_call(
        functools.partial(up_kernel, sections, shots, group, sizes),
        out_shape=[
            jax.ShapeDtypeStruct((slots * rows + TAIL * more, columns), bf16)
            for more in (0, 1, 0, 2)
        ]
        + buffers,
        in_specs=[vmem] * 12,
        out_specs=[vmem] * (sections + 4),
        scratch_shapes=stages
        + [pltpu.VMEM((2 * rows, columns), bf16), pltpu.SMEM((sections,), jnp.int32)],
        input_output_aliases={8 + i: sections + i for i in range(4)},
        compiler_params=params(24),
        name="up",
    )(
        *messages, late, *[held(part) for part in lates], joined, far_window,
        *[held(buffer) for buffer in filled],
    )

    corr_shape = jax.ShapeDtypeStruct((slots * rows, columns), bf16)
    arrived = [correlations[0]] + [
        lax.ppermute(correlations[r], BOTH, plan.from_workers(r)) for r in range(1, sections)
    ]
    left, own = pl.pallas_call(
        functools.partial(place_kernel, shots),
        out_shape=[corr_shape, jax.ShapeDtypeStruct((slots * rows, columns), jnp.float32)],
        in_specs=[vmem] * (1 + sections),
        out_specs=[vmem, vmem],
        compiler_params=params(8),
        name="place",
    )(held(shifts), *[held(part) for part in arrived])
    from_right = lax.ppermute(left, "tile", [(i + 1, i) for i in range(plan.tiles - 1)])
    image = own + from_right.astype(jnp.float32)
    return image.reshape(1, slots, rows, columns)


def solution(mesh):
    return jax.shard_map(
        on_device,
        mesh=mesh,
        in_specs=(
            P("tile", None, None, None),
            P("tile"),
            P("depth"),
            P("depth", None, None, "tile"),
            P("depth", None, None, None, None),
            P("depth", None, None, None, None),
        ),
        out_specs=P("depth", None, None, "tile"),
        check_vma=False,
    )
```

profile of v0, /device:TPU:1, one launch (start us, length us, event | category | flops | bytes accessed | tf_op | source)
XLA Modules:
  0.0 55.4 jit_solution(4950711704365054858)
XLA Ops:
  0.0 4.6 %collective-permute-start.2 = (bf16[384,256]{1,0:T(8,128)(2,1)}, bf16[384,256]{1,0:T(8,128)(2,1)S(1)}, u32[]{:S(2)}, u32[]{:S(2)}) collective-permute-start(bf16[384,256]{1,0:T(8,128)(2,1)} %bitcast.8), channel_id=1, source_target_pairs={{0,1},{1,2},{2,3},{3,4},{4,5},{5,6},{6,7},{8,9},{9,10},{10,11},{11... | collective-permute-start | bytes 589832 | tf_op jit(solution)/shard_map/ppermute | solution.py:360
  4.6 1.4 %pack.1 = (bf16[1760,256]{1,0:T(8,128)(2,1)S(1)}, bf16[1680,256]{1,0:T(8,128)(2,1)S(1)}, bf16[640,256]{1,0:T(8,128)(2,1)S(1)}, bf16[960,256]{1,0:T(8,128)(2,1)S(1)}) custom-call(bf16[3,2,128,128]{3,2,1,0:T(8,128)(2,1)} %bitcast.7, bf16[3,2,256,256]{3,2,1,0:T(8,128)(2,1)} %bitcast.6), custom_call_target="tpu_custom_call" | custom-call | tf_op jit(solution)/shard_map/pack/pallas_call | solution.py:366
  6.0 4.1 %collective-permute-start = (bf16[960,256]{1,0:T(8,128)(2,1)S(1)}, bf16[960,256]{1,0:T(8,128)(2,1)S(1)}, u32[]{:S(2)}, u32[]{:S(2)}) collective-permute-start(bf16[960,256]{1,0:T(8,128)(2,1)S(1)} %get-tuple-element.24), channel_id=1, source_target_pairs={{24,0},{16,8},{9,17},{1,25},{26,2},{18,10},{11,19},{3,27},{28,4},{... | collective-permute-start | bytes 1474568 | tf_op jit(solution)/shard_map/ppermute | solution.py:385
  10.8 0.0 collective-permute-done.2.left_ref
  10.8 1.2 %windows.1 = (bf16[1760,256]{1,0:T(8,128)(2,1)S(1)}, bf16[1680,256]{1,0:T(8,128)(2,1)S(1)}, bf16[400,256]{1,0:T(8,128)(2,1)S(1)}) custom-call(s32[2]{0:T(128)} %anchors_hbm.1, s32[1]{0:T(128)S(6)} %copy.21.counts, bf16[384,256]{1,0:T(8,128)(2,1)S(1)} %collective-permute-done.2.left_ref, ...), custom_call_target="tpu_custom_call", output_to_operand_aliasing={{0}: (4, {}), {1}: (5, {})} | custom-call | flops 3000000000 | bytes 4194304 | tf_op jit(solution)/shard_map/windows/pallas_call | solution.py:386
  12.0 1.3 %collective-permute-start.4 = (bf16[1760,256]{1,0:T(8,128)(2,1)S(1)}, bf16[1760,256]{1,0:T(8,128)(2,1)S(1)}, u32[]{:S(2)}, u32[]{:S(2)}) collective-permute-start(bf16[1760,256]{1,0:T(8,128)(2,1)S(1)} %get-tuple-element.28.refs_0_), channel_id=1, source_target_pairs={{16,0},{24,8},{1,17},{9,25},{18,2},{26,10},{3,19},{11,27},{20,4},{... | collective-permute-start | bytes 2703368 | tf_op jit(solution)/shard_map/ppermute | solution.py:404
  13.3 1.3 %collective-permute-start.5 = (bf16[400,256]{1,0:T(8,128)(2,1)S(1)}, bf16[400,256]{1,0:T(8,128)(2,1)S(1)}, u32[]{:S(2)}, u32[]{:S(2)}) collective-permute-start(bf16[400,256]{1,0:T(8,128)(2,1)S(1)} %get-tuple-element.31), channel_id=1, source_target_pairs={{24,0},{16,8},{9,17},{1,25},{26,2},{18,10},{11,19},{3,27},{28,4},{... | collective-permute-start | bytes 614408 | tf_op jit(solution)/shard_map/ppermute | solution.py:406
  14.6 0.7 %collective-permute-start.3 = (bf16[1680,256]{1,0:T(8,128)(2,1)S(1)}, bf16[1680,256]{1,0:T(8,128)(2,1)S(1)}, u32[]{:S(2)}, u32[]{:S(2)}) collective-permute-start(bf16[1680,256]{1,0:T(8,128)(2,1)S(1)} %get-tuple-element.29), channel_id=1, source_target_pairs={{8,0},{0,8},{25,17},{17,25},{10,2},{2,10},{27,19},{19,27},{12,4},{... | collective-permute-start | bytes 2580488 | tf_op jit(solution)/shard_map/ppermute | solution.py:403
  15.4 1.8 %collective-permute-done.first_ref = bf16[960,256]{1,0:T(8,128)(2,1)S(1)} collective-permute-done((bf16[960,256]{1,0:T(8,128)(2,1)S(1)}, bf16[960,256]{1,0:T(8,128)(2,1)S(1)}, u32[]{:S(2)}, u32[]{:S(2)}) %collective-permute-start) | collective-permute-done | bytes 491552 | tf_op jit(solution)/shard_map/ppermute | solution.py:385
  17.1 0.7 %collective-permute-start.1 = (bf16[960,256]{1,0:T(8,128)(2,1)S(1)}, bf16[960,256]{1,0:T(8,128)(2,1)S(1)}, u32[]{:S(2)}, u32[]{:S(2)}) collective-permute-start(bf16[960,256]{1,0:T(8,128)(2,1)S(1)} %collective-permute-done.first_ref), channel_id=1, source_target_pairs={{0,2},{8,10},{17,19},{25,27},{2,0},{10,8},{19,17},{27,25},{4,6},{1... | collective-permute-start | bytes 1474568 | tf_op jit(solution)/shard_map/ppermute | solution.py:407
  17.8 3.7 %collective-permute-done.5.after_ref.refs_5_.refs_7_ = bf16[400,256]{1,0:T(8,128)(2,1)S(1)} collective-permute-done((bf16[400,256]{1,0:T(8,128)(2,1)S(1)}, bf16[400,256]{1,0:T(8,128)(2,1)S(1)}, u32[]{:S(2)}, u32[]{:S(2)}) %collective-permute-start.5) | collective-permute-done | bytes 204832 | tf_op jit(solution)/shard_map/ppermute | solution.py:406
  21.5 0.0 copy-start
  21.5 4.4 %collective-permute-start.7 = (bf16[640,256]{1,0:T(8,128)(2,1)S(1)}, bf16[640,256]{1,0:T(8,128)(2,1)S(1)}, u32[]{:S(2)}, u32[]{:S(2)}) collective-permute-start(bf16[640,256]{1,0:T(8,128)(2,1)S(1)} %hold.1.refs_3_), channel_id=1, source_target_pairs={{16,0},{24,8},{1,17},{9,25},{18,2},{26,10},{3,19},{11,27},{20,4},{... | collective-permute-start | bytes 983048 | tf_op jit(solution)/shard_map/ppermute | solution.py:418
  26.0 1.3 %collective-permute-start.6 = (bf16[640,256]{1,0:T(8,128)(2,1)S(1)}, bf16[640,256]{1,0:T(8,128)(2,1)S(1)}, u32[]{:S(2)}, u32[]{:S(2)}) collective-permute-start(bf16[640,256]{1,0:T(8,128)(2,1)S(1)} %hold.1.refs_3_), channel_id=1, source_target_pairs={{9,0},{1,8},{24,17},{16,25},{11,2},{3,10},{26,19},{18,27},{13,4},{... | collective-permute-start | bytes 983048 | tf_op jit(solution)/shard_map/ppermute | solution.py:418
  27.3 0.0 collective-permute-done.1.second_ref
  27.3 0.0 copy-done.1
  27.3 0.7 %join.1 = (bf16[1920,256]{1,0:T(8,128)(2,1)S(1)}, bf16[2,256,512]{2,1,0:T(8,128)(2,1)S(1)}) custom-call(s32[2]{0:T(128)S(1)} %copy-done.1, bf16[960,256]{1,0:T(8,128)(2,1)S(1)} %collective-permute-done.first_ref, bf16[960,256]{1,0:T(8,128)(2,1)S(1)} %collective-permute-done.1.second_ref), custom_call_target="tpu_custom_call" | custom-call | tf_op jit(solution)/shard_map/join/pallas_call | solution.py:419
  28.0 0.0 collective-permute-done.3.refs_1_
  28.0 0.0 collective-permute-done.4.refs_2_
  28.1 0.0 copy-done
  28.1 3.1 %collective-permute-done.7.refs_5_ = bf16[640,256]{1,0:T(8,128)(2,1)S(1)} collective-permute-done((bf16[640,256]{1,0:T(8,128)(2,1)S(1)}, bf16[640,256]{1,0:T(8,128)(2,1)S(1)}, u32[]{:S(2)}, u32[]{:S(2)}) %collective-permute-start.7) | collective-permute-done | bytes 327712 | tf_op jit(solution)/shard_map/ppermute | solution.py:418
  31.2 0.1 collective-permute-done.6.refs_4_
  31.3 1.3 %collective-permute-start.10 = (bf16[416,256]{1,0:T(8,128)(2,1)S(1)}, bf16[416,256]{1,0:T(8,128)(2,1)S(1)}, u32[]{:S(2)}, u32[]{:S(2)}) collective-permute-start(bf16[416,256]{1,0:T(8,128)(2,1)S(1)} %get-tuple-element.40), channel_id=1, source_target_pairs={{0,24},{8,16},{17,9},{25,1},{2,26},{10,18},{19,11},{27,3},{4,28},{... | collective-permute-start | bytes 638984 | tf_op jit(solution)/shard_map/ppermute | solution.py:471
  32.6 0.7 %collective-permute-start.8 = (bf16[400,256]{1,0:T(8,128)(2,1)S(1)}, bf16[400,256]{1,0:T(8,128)(2,1)S(1)}, u32[]{:S(2)}, u32[]{:S(2)}) collective-permute-start(bf16[400,256]{1,0:T(8,128)(2,1)S(1)} %get-tuple-element.38), channel_id=1, source_target_pairs={{0,8},{8,0},{17,25},{25,17},{2,10},{10,2},{19,27},{27,19},{4,12},{... | collective-permute-start | bytes 614408 | tf_op jit(solution)/shard_map/ppermute | solution.py:471
  33.3 1.3 %collective-permute-start.9 = (bf16[384,256]{1,0:T(8,128)(2,1)S(1)}, bf16[384,256]{1,0:T(8,128)(2,1)S(1)}, u32[]{:S(2)}, u32[]{:S(2)}) collective-permute-start(bf16[384,256]{1,0:T(8,128)(2,1)S(1)} %get-tuple-element.39), channel_id=1, source_target_pairs={{0,16},{8,24},{17,1},{25,9},{2,18},{10,26},{19,3},{27,11},{4,20},{... | collective-permute-start | bytes 589832 | tf_op jit(solution)/shard_map/ppermute | solution.py:471
  34.6 12.7 %collective-permute-done.9.refs_2_ = bf16[384,256]{1,0:T(8,128)(2,1)S(1)} collective-permute-done((bf16[384,256]{1,0:T(8,128)(2,1)S(1)}, bf16[384,256]{1,0:T(8,128)(2,1)S(1)}, u32[]{:S(2)}, u32[]{:S(2)}) %collective-permute-start.9) | collective-permute-done | bytes 196640 | tf_op jit(solution)/shard_map/ppermute | solution.py:471
  47.3 0.0 collective-permute-done.8.refs_1_
  47.3 0.0 collective-permute-done.10.refs_3_
  47.3 0.4 place.1
  47.6 2.0 %collective-permute-start.11 = (bf16[384,256]{1,0:T(8,128)(2,1)S(1)}, bf16[384,256]{1,0:T(8,128)(2,1)S(1)}, u32[]{:S(2)}, u32[]{:S(2)}) collective-permute-start(bf16[384,256]{1,0:T(8,128)(2,1)S(1)} %get-tuple-element.42), channel_id=1, source_target_pairs={{1,0},{2,1},{3,2},{4,3},{5,4},{6,5},{7,6},{9,8},{10,9},{11,10},{12... | collective-permute-start | bytes 589832 | tf_op jit(solution)/shard_map/ppermute | solution.py:481
  49.6 5.0 %collective-permute-done.11 = bf16[384,256]{1,0:T(8,128)(2,1)S(1)} collective-permute-done((bf16[384,256]{1,0:T(8,128)(2,1)S(1)}, bf16[384,256]{1,0:T(8,128)(2,1)S(1)}, u32[]{:S(2)}, u32[]{:S(2)}) %collective-permute-start.11) | collective-permute-done | bytes 196640 | tf_op jit(solution)/shard_map/ppermute | solution.py:481
  54.6 0.8 %convert_add_fusion = f32[384,256]{1,0:T(8,128)} fusion(f32[384,256]{1,0:T(8,128)S(1)} %get-tuple-element.41, bf16[384,256]{1,0:T(8,128)(2,1)S(1)} %collective-permute-done.11), kind=kLoop, calls=%fused_computation | loop fusion | flops 196608 | bytes 983040 | tf_op jit(solution)/shard_map/add | solution.py:482
  (4 shorter events, 0.0 us)
Async XLA Ops:
  0.0 10.8 %collective-permute-start.2 = (bf16[384,256]{1,0:T(8,128)(2,1)}, bf16[384,256]{1,0:T(8,128)(2,1)S(1)}, u32[]{:S(2)}, u32[]{:S(2)}) collective-permute-start(bf16[384,256]{1,0:T(8,128)(2,1)} %bitcast.8), channel_id=1, source_target_pairs={{0,1},{1,2},{2,3},{3,4},{4,5},{5,6},{6,7},{8,9},{9,10},{10,11},{11... | collective-permute-start | bytes 589832 | tf_op jit(solution)/shard_map/ppermute | solution.py:360
  6.0 11.1 %collective-permute-start = (bf16[960,256]{1,0:T(8,128)(2,1)S(1)}, bf16[960,256]{1,0:T(8,128)(2,1)S(1)}, u32[]{:S(2)}, u32[]{:S(2)}) collective-permute-start(bf16[960,256]{1,0:T(8,128)(2,1)S(1)} %get-tuple-element.24), channel_id=1, source_target_pairs={{24,0},{16,8},{9,17},{1,25},{26,2},{18,10},{11,19},{3,27},{28,4},{... | collective-permute-start | bytes 1474568 | tf_op jit(solution)/shard_map/ppermute | solution.py:385
  12.0 16.1 %collective-permute-start.4 = (bf16[1760,256]{1,0:T(8,128)(2,1)S(1)}, bf16[1760,256]{1,0:T(8,128)(2,1)S(1)}, u32[]{:S(2)}, u32[]{:S(2)}) collective-permute-start(bf16[1760,256]{1,0:T(8,128)(2,1)S(1)} %get-tuple-element.28.refs_0_), channel_id=1, source_target_pairs={{16,0},{24,8},{1,17},{9,25},{18,2},{26,10},{3,19},{11,27},{20,4},{... | collective-permute-start | bytes 2703368 | tf_op jit(solution)/shard_map/ppermute | solution.py:404
  13.3 8.2 %collective-permute-start.5 = (bf16[400,256]{1,0:T(8,128)(2,1)S(1)}, bf16[400,256]{1,0:T(8,128)(2,1)S(1)}, u32[]{:S(2)}, u32[]{:S(2)}) collective-permute-start(bf16[400,256]{1,0:T(8,128)(2,1)S(1)} %get-tuple-element.31), channel_id=1, source_target_pairs={{24,0},{16,8},{9,17},{1,25},{26,2},{18,10},{11,19},{3,27},{28,4},{... | collective-permute-start | bytes 614408 | tf_op jit(solution)/shard_map/ppermute | solution.py:406
  14.6 13.4 %collective-permute-start.3 = (bf16[1680,256]{1,0:T(8,128)(2,1)S(1)}, bf16[1680,256]{1,0:T(8,128)(2,1)S(1)}, u32[]{:S(2)}, u32[]{:S(2)}) collective-permute-start(bf16[1680,256]{1,0:T(8,128)(2,1)S(1)} %get-tuple-element.29), channel_id=1, source_target_pairs={{8,0},{0,8},{25,17},{17,25},{10,2},{2,10},{27,19},{19,27},{12,4},{... | collective-permute-start | bytes 2580488 | tf_op jit(solution)/shard_map/ppermute | solution.py:403
  17.1 10.1 %collective-permute-start.1 = (bf16[960,256]{1,0:T(8,128)(2,1)S(1)}, bf16[960,256]{1,0:T(8,128)(2,1)S(1)}, u32[]{:S(2)}, u32[]{:S(2)}) collective-permute-start(bf16[960,256]{1,0:T(8,128)(2,1)S(1)} %collective-permute-done.first_ref), channel_id=1, source_target_pairs={{0,2},{8,10},{17,19},{25,27},{2,0},{10,8},{19,17},{27,25},{4,6},{1... | collective-permute-start | bytes 1474568 | tf_op jit(solution)/shard_map/ppermute | solution.py:407
  21.5 5.7 %copy-start.1 = (s32[2]{0:T(128)S(1)}, s32[2]{0:T(128)}, u32[]{:S(2)}) copy-start(s32[2]{0:T(128)} %anchors_hbm.1) | copy-start | bytes 28
  21.5 6.5 %copy-start = (bf16[2,2,128,256]{3,2,1,0:T(8,128)(2,1)S(1)}, bf16[2,2,128,256]{3,2,1,0:T(8,128)(2,1)}, u32[]{:S(2)}) copy-start(bf16[2,2,128,256]{3,2,1,0:T(8,128)(2,1)} %param.6) | copy-start | bytes 786436
  21.5 9.6 %collective-permute-start.7 = (bf16[640,256]{1,0:T(8,128)(2,1)S(1)}, bf16[640,256]{1,0:T(8,128)(2,1)S(1)}, u32[]{:S(2)}, u32[]{:S(2)}) collective-permute-start(bf16[640,256]{1,0:T(8,128)(2,1)S(1)} %hold.1.refs_3_), channel_id=1, source_target_pairs={{16,0},{24,8},{1,17},{9,25},{18,2},{26,10},{3,19},{11,27},{20,4},{... | collective-permute-start | bytes 983048 | tf_op jit(solution)/shard_map/ppermute | solution.py:418
  26.0 5.3 %collective-permute-start.6 = (bf16[640,256]{1,0:T(8,128)(2,1)S(1)}, bf16[640,256]{1,0:T(8,128)(2,1)S(1)}, u32[]{:S(2)}, u32[]{:S(2)}) collective-permute-start(bf16[640,256]{1,0:T(8,128)(2,1)S(1)} %hold.1.refs_3_), channel_id=1, source_target_pairs={{9,0},{1,8},{24,17},{16,25},{11,2},{3,10},{26,19},{18,27},{13,4},{... | collective-permute-start | bytes 983048 | tf_op jit(solution)/shard_map/ppermute | solution.py:418
  31.3 16.0 %collective-permute-start.10 = (bf16[416,256]{1,0:T(8,128)(2,1)S(1)}, bf16[416,256]{1,0:T(8,128)(2,1)S(1)}, u32[]{:S(2)}, u32[]{:S(2)}) collective-permute-start(bf16[416,256]{1,0:T(8,128)(2,1)S(1)} %get-tuple-element.40), channel_id=1, source_target_pairs={{0,24},{8,16},{17,9},{25,1},{2,26},{10,18},{19,11},{27,3},{4,28},{... | collective-permute-start | bytes 638984 | tf_op jit(solution)/shard_map/ppermute | solution.py:471
  32.6 14.7 %collective-permute-start.8 = (bf16[400,256]{1,0:T(8,128)(2,1)S(1)}, bf16[400,256]{1,0:T(8,128)(2,1)S(1)}, u32[]{:S(2)}, u32[]{:S(2)}) collective-permute-start(bf16[400,256]{1,0:T(8,128)(2,1)S(1)} %get-tuple-element.38), channel_id=1, source_target_pairs={{0,8},{8,0},{17,25},{25,17},{2,10},{10,2},{19,27},{27,19},{4,12},{... | collective-permute-start | bytes 614408 | tf_op jit(solution)/shard_map/ppermute | solution.py:471
  33.3 14.0 %collective-permute-start.9 = (bf16[384,256]{1,0:T(8,128)(2,1)S(1)}, bf16[384,256]{1,0:T(8,128)(2,1)S(1)}, u32[]{:S(2)}, u32[]{:S(2)}) collective-permute-start(bf16[384,256]{1,0:T(8,128)(2,1)S(1)} %get-tuple-element.39), channel_id=1, source_target_pairs={{0,16},{8,24},{17,1},{25,9},{2,18},{10,26},{19,3},{27,11},{4,20},{... | collective-permute-start | bytes 589832 | tf_op jit(solution)/shard_map/ppermute | solution.py:471
  47.6 7.0 %collective-permute-start.11 = (bf16[384,256]{1,0:T(8,128)(2,1)S(1)}, bf16[384,256]{1,0:T(8,128)(2,1)S(1)}, u32[]{:S(2)}, u32[]{:S(2)}) collective-permute-start(bf16[384,256]{1,0:T(8,128)(2,1)S(1)} %get-tuple-element.42), channel_id=1, source_target_pairs={{1,0},{2,1},{3,2},{4,3},{5,4},{6,5},{7,6},{9,8},{10,9},{11,10},{12... | collective-permute-start | bytes 589832 | tf_op jit(solution)/shard_map/ppermute | solution.py:481
where the time goes:
time: 54.9 us; the launch traced here: 55.4 us
  waiting for transfers between devices  26.3 us (48%)
  starting transfers between devices  23.7 us (43%)
  Pallas kernels  3.76 us (7%)
  between operations  0.84 us (2%)
  other arithmetic  0.78 us (1%)
    ppermute x3, waiting for transfers between devices, on_device(): lax.ppermute(correlations[r], BOTH, plan.from_workers(r))  12.7 us
    ppermute x2, starting transfers between devices, on_device(): lates = [lax.ppermute(late, BOTH, plan.ops_to_workers(r)) for r in (1, 2)]  5.71 us
    ppermute x1, waiting for transfers between devices, on_device(): lax.ppermute(left, 'tile', [(i + 1, i) for i in range(plan.tiles - 1)])  5.01 us
    ppermute x1, starting transfers between devices, on_device(): lax.ppermute(tile_reflect, 'tile', [(i, i + 1) for i in range(plan.tiles...  4.58 us
    ppermute x1, starting transfers between devices, on_device(): far_half = lax.ppermute(far_half, BOTH, plan.to_workers(last))  4.1 us
    ppermute x1, waiting for transfers between devices, on_device(): far_window = lax.ppermute(far_window, BOTH, plan.to_workers(last))  3.7 us
    ppermute x3, starting transfers between devices, on_device(): lax.ppermute(correlations[r], BOTH, plan.from_workers(r))  3.26 us
    ppermute x2, waiting for transfers between devices, on_device(): lates = [lax.ppermute(late, BOTH, plan.ops_to_workers(r)) for r in (1, 2)]  3.15 us
  transfers between devices with their start and end apart: 12, of which 6 were waited for; matrix products, arithmetic and copies ran while one was open for 0% of the time, Pallas kernels for 6%

commit v1 on v0

--- a/solution.py
+++ b/solution.py
@@ -451,7 +451,7 @@
         functools.partial(up_kernel, sections, shots, group, sizes),
         out_shape=[
             jax.ShapeDtypeStruct((slots * rows + TAIL * more, columns), bf16)
-            for more in (0, 1, 0, 2)
+            for more in (0, 0, 1, 2)
         ]
         + buffers,
         in_specs=[vmem] * 12,

time: 54.9 us -> 56 us (1.020); the launches traced: 55.4 us -> 55.6 us
  starting transfers between devices: 23.7 us -> 26.1 us
  waiting for transfers between devices: 26.3 us -> 24.1 us
    ppermute x1, starting transfers between devices: 1.97 us -> 4.37 us  [on_device(): lax.ppermute(left, 'tile', [(i + 1, i) for i in range(plan.tiles - 1)])]
    ppermute x3, waiting for transfers between devices: 12.7 us -> 11.4 us  [on_device(): lax.ppermute(correlations[r], BOTH, plan.from_workers(r))]
    ppermute x1, waiting for transfers between devices: 5.01 us -> 4.08 us  [on_device(): lax.ppermute(left, 'tile', [(i + 1, i) for i in range(plan.tiles - 1)])]
where the time goes in v1:
time: 56 us; the launch traced here: 55.6 us
  starting transfers between devices  26.1 us (47%)
  waiting for transfers between devices  24.1 us (43%)
  Pallas kernels  3.76 us (7%)
  between operations  0.85 us (2%)
  other arithmetic  0.78 us (1%)
    ppermute x3, waiting for transfers between devices, on_device(): lax.ppermute(correlations[r], BOTH, plan.from_workers(r))  11.4 us
    ppermute x2, starting transfers between devices, on_device(): lates = [lax.ppermute(late, BOTH, plan.ops_to_workers(r)) for r in (1, 2)]  5.71 us
    ppermute x1, starting transfers between devices, on_device(): lax.ppermute(tile_reflect, 'tile', [(i, i + 1) for i in range(plan.tiles...  4.58 us
    ppermute x1, starting transfers between devices, on_device(): lax.ppermute(left, 'tile', [(i + 1, i) for i in range(plan.tiles - 1)])  4.37 us
    ppermute x1, starting transfers between devices, on_device(): far_half = lax.ppermute(far_half, BOTH, plan.to_workers(last))  4.1 us
    ppermute x1, waiting for transfers between devices, on_device(): lax.ppermute(left, 'tile', [(i + 1, i) for i in range(plan.tiles - 1)])  4.08 us
    ppermute x1, waiting for transfers between devices, on_device(): far_window = lax.ppermute(far_window, BOTH, plan.to_workers(last))  3.7 us
    ppermute x3, starting transfers between devices, on_device(): lax.ppermute(correlations[r], BOTH, plan.from_workers(r))  3.26 us
  transfers between devices with their start and end apart: 12, of which 6 were waited for; matrix products, arithmetic and copies ran while one was open for 0% of the time, Pallas kernels for 6%

profile of v1, /device:TPU:1, one launch (start us, length us, event | category | flops | bytes accessed | tf_op | source)
XLA Modules:
  0.0 55.6 jit_solution(3028584747988098599)
XLA Ops:
  0.0 4.6 %collective-permute-start.2 = (bf16[384,256]{1,0:T(8,128)(2,1)}, bf16[384,256]{1,0:T(8,128)(2,1)S(1)}, u32[]{:S(2)}, u32[]{:S(2)}) collective-permute-start(bf16[384,256]{1,0:T(8,128)(2,1)} %bitcast.8), channel_id=1, source_target_pairs={{0,1},{1,2},{2,3},{3,4},{4,5},{5,6},{6,7},{8,9},{9,10},{10,11},{11... | collective-permute-start | bytes 589832 | tf_op jit(solution)/shard_map/ppermute | solution.py:360
  4.6 1.4 %pack.1 = (bf16[1760,256]{1,0:T(8,128)(2,1)S(1)}, bf16[1680,256]{1,0:T(8,128)(2,1)S(1)}, bf16[640,256]{1,0:T(8,128)(2,1)S(1)}, bf16[960,256]{1,0:T(8,128)(2,1)S(1)}) custom-call(bf16[3,2,128,128]{3,2,1,0:T(8,128)(2,1)} %bitcast.7, bf16[3,2,256,256]{3,2,1,0:T(8,128)(2,1)} %bitcast.6), custom_call_target="tpu_custom_call" | custom-call | tf_op jit(solution)/shard_map/pack/pallas_call | solution.py:366
  6.0 4.1 %collective-permute-start = (bf16[960,256]{1,0:T(8,128)(2,1)S(1)}, bf16[960,256]{1,0:T(8,128)(2,1)S(1)}, u32[]{:S(2)}, u32[]{:S(2)}) collective-permute-start(bf16[960,256]{1,0:T(8,128)(2,1)S(1)} %get-tuple-element.24), channel_id=1, source_target_pairs={{24,0},{16,8},{9,17},{1,25},{26,2},{18,10},{11,19},{3,27},{28,4},{... | collective-permute-start | bytes 1474568 | tf_op jit(solution)/shard_map/ppermute | solution.py:385
  10.8 0.0 collective-permute-done.2.left_ref
  10.8 1.2 %windows.1 = (bf16[1760,256]{1,0:T(8,128)(2,1)S(1)}, bf16[1680,256]{1,0:T(8,128)(2,1)S(1)}, bf16[400,256]{1,0:T(8,128)(2,1)S(1)}) custom-call(s32[2]{0:T(128)} %anchors_hbm.1, s32[1]{0:T(128)S(6)} %copy.21.counts, bf16[384,256]{1,0:T(8,128)(2,1)S(1)} %collective-permute-done.2.left_ref, ...), custom_call_target="tpu_custom_call", output_to_operand_aliasing={{0}: (4, {}), {1}: (5, {})} | custom-call | flops 3000000000 | bytes 4194304 | tf_op jit(solution)/shard_map/windows/pallas_call | solution.py:386
  12.0 1.3 %collective-permute-start.4 = (bf16[1760,256]{1,0:T(8,128)(2,1)S(1)}, bf16[1760,256]{1,0:T(8,128)(2,1)S(1)}, u32[]{:S(2)}, u32[]{:S(2)}) collective-permute-start(bf16[1760,256]{1,0:T(8,128)(2,1)S(1)} %get-tuple-element.28.refs_0_), channel_id=1, source_target_pairs={{16,0},{24,8},{1,17},{9,25},{18,2},{26,10},{3,19},{11,27},{20,4},{... | collective-permute-start | bytes 2703368 | tf_op jit(solution)/shard_map/ppermute | solution.py:404
  13.3 1.3 %collective-permute-start.5 = (bf16[400,256]{1,0:T(8,128)(2,1)S(1)}, bf16[400,256]{1,0:T(8,128)(2,1)S(1)}, u32[]{:S(2)}, u32[]{:S(2)}) collective-permute-start(bf16[400,256]{1,0:T(8,128)(2,1)S(1)} %get-tuple-element.31), channel_id=1, source_target_pairs={{24,0},{16,8},{9,17},{1,25},{26,2},{18,10},{11,19},{3,27},{28,4},{... | collective-permute-start | bytes 614408 | tf_op jit(solution)/shard_map/ppermute | solution.py:406
  14.6 0.7 %collective-permute-start.3 = (bf16[1680,256]{1,0:T(8,128)(2,1)S(1)}, bf16[1680,256]{1,0:T(8,128)(2,1)S(1)}, u32[]{:S(2)}, u32[]{:S(2)}) collective-permute-start(bf16[1680,256]{1,0:T(8,128)(2,1)S(1)} %get-tuple-element.29), channel_id=1, source_target_pairs={{8,0},{0,8},{25,17},{17,25},{10,2},{2,10},{27,19},{19,27},{12,4},{... | collective-permute-start | bytes 2580488 | tf_op jit(solution)/shard_map/ppermute | solution.py:403
  15.4 1.8 %collective-permute-done.first_ref = bf16[960,256]{1,0:T(8,128)(2,1)S(1)} collective-permute-done((bf16[960,256]{1,0:T(8,128)(2,1)S(1)}, bf16[960,256]{1,0:T(8,128)(2,1)S(1)}, u32[]{:S(2)}, u32[]{:S(2)}) %collective-permute-start) | collective-permute-done | bytes 491552 | tf_op jit(solution)/shard_map/ppermute | solution.py:385
  17.1 0.7 %collective-permute-start.1 = (bf16[960,256]{1,0:T(8,128)(2,1)S(1)}, bf16[960,256]{1,0:T(8,128)(2,1)S(1)}, u32[]{:S(2)}, u32[]{:S(2)}) collective-permute-start(bf16[960,256]{1,0:T(8,128)(2,1)S(1)} %collective-permute-done.first_ref), channel_id=1, source_target_pairs={{0,2},{8,10},{17,19},{25,27},{2,0},{10,8},{19,17},{27,25},{4,6},{1... | collective-permute-start | bytes 1474568 | tf_op jit(solution)/shard_map/ppermute | solution.py:407
  17.8 3.7 %collective-permute-done.5.after_ref.refs_5_.refs_7_ = bf16[400,256]{1,0:T(8,128)(2,1)S(1)} collective-permute-done((bf16[400,256]{1,0:T(8,128)(2,1)S(1)}, bf16[400,256]{1,0:T(8,128)(2,1)S(1)}, u32[]{:S(2)}, u32[]{:S(2)}) %collective-permute-start.5) | collective-permute-done | bytes 204832 | tf_op jit(solution)/shard_map/ppermute | solution.py:406
  21.5 0.0 copy-start.1
  21.5 4.4 %collective-permute-start.7 = (bf16[640,256]{1,0:T(8,128)(2,1)S(1)}, bf16[640,256]{1,0:T(8,128)(2,1)S(1)}, u32[]{:S(2)}, u32[]{:S(2)}) collective-permute-start(bf16[640,256]{1,0:T(8,128)(2,1)S(1)} %hold.1.refs_3_), channel_id=1, source_target_pairs={{16,0},{24,8},{1,17},{9,25},{18,2},{26,10},{3,19},{11,27},{20,4},{... | collective-permute-start | bytes 983048 | tf_op jit(solution)/shard_map/ppermute | solution.py:418
  26.0 1.3 %collective-permute-start.6 = (bf16[640,256]{1,0:T(8,128)(2,1)S(1)}, bf16[640,256]{1,0:T(8,128)(2,1)S(1)}, u32[]{:S(2)}, u32[]{:S(2)}) collective-permute-start(bf16[640,256]{1,0:T(8,128)(2,1)S(1)} %hold.1.refs_3_), channel_id=1, source_target_pairs={{9,0},{1,8},{24,17},{16,25},{11,2},{3,10},{26,19},{18,27},{13,4},{... | collective-permute-start | bytes 983048 | tf_op jit(solution)/shard_map/ppermute | solution.py:418
  27.3 0.0 collective-permute-done.1.second_ref
  27.3 0.0 copy-done.1
  27.3 0.7 %join.1 = (bf16[1920,256]{1,0:T(8,128)(2,1)S(1)}, bf16[2,256,512]{2,1,0:T(8,128)(2,1)S(1)}) custom-call(s32[2]{0:T(128)S(1)} %copy-done.1, bf16[960,256]{1,0:T(8,128)(2,1)S(1)} %collective-permute-done.first_ref, bf16[960,256]{1,0:T(8,128)(2,1)S(1)} %collective-permute-done.1.second_ref), custom_call_target="tpu_custom_call" | custom-call | tf_op jit(solution)/shard_map/join/pallas_call | solution.py:419
  28.0 0.0 collective-permute-done.3.refs_1_
  28.0 0.0 collective-permute-done.4.refs_2_
  28.1 0.0 copy-done
  28.1 3.1 %collective-permute-done.7.refs_5_ = bf16[640,256]{1,0:T(8,128)(2,1)S(1)} collective-permute-done((bf16[640,256]{1,0:T(8,128)(2,1)S(1)}, bf16[640,256]{1,0:T(8,128)(2,1)S(1)}, u32[]{:S(2)}, u32[]{:S(2)}) %collective-permute-start.7) | collective-permute-done | bytes 327712 | tf_op jit(solution)/shard_map/ppermute | solution.py:418
  31.2 0.1 collective-permute-done.6.refs_4_
  31.3 1.3 %collective-permute-start.10 = (bf16[416,256]{1,0:T(8,128)(2,1)S(1)}, bf16[416,256]{1,0:T(8,128)(2,1)S(1)}, u32[]{:S(2)}, u32[]{:S(2)}) collective-permute-start(bf16[416,256]{1,0:T(8,128)(2,1)S(1)} %get-tuple-element.40), channel_id=1, source_target_pairs={{0,24},{8,16},{17,9},{25,1},{2,26},{10,18},{19,11},{27,3},{4,28},{... | collective-permute-start | bytes 638984 | tf_op jit(solution)/shard_map/ppermute | solution.py:471
  32.6 1.3 %collective-permute-start.9 = (bf16[400,256]{1,0:T(8,128)(2,1)S(1)}, bf16[400,256]{1,0:T(8,128)(2,1)S(1)}, u32[]{:S(2)}, u32[]{:S(2)}) collective-permute-start(bf16[400,256]{1,0:T(8,128)(2,1)S(1)} %get-tuple-element.39), channel_id=1, source_target_pairs={{0,16},{8,24},{17,1},{25,9},{2,18},{10,26},{19,3},{27,11},{4,20},{... | collective-permute-start | bytes 614408 | tf_op jit(solution)/shard_map/ppermute | solution.py:471
  33.9 0.7 %collective-permute-start.8 = (bf16[384,256]{1,0:T(8,128)(2,1)S(1)}, bf16[384,256]{1,0:T(8,128)(2,1)S(1)}, u32[]{:S(2)}, u32[]{:S(2)}) collective-permute-start(bf16[384,256]{1,0:T(8,128)(2,1)S(1)} %get-tuple-element.38), channel_id=1, source_target_pairs={{0,8},{8,0},{17,25},{25,17},{2,10},{10,2},{19,27},{27,19},{4,12},{... | collective-permute-start | bytes 589832 | tf_op jit(solution)/shard_map/ppermute | solution.py:471
  34.6 0.0 collective-permute-done.8.refs_1_
  34.6 11.4 %collective-permute-done.9.refs_2_ = bf16[400,256]{1,0:T(8,128)(2,1)S(1)} collective-permute-done((bf16[400,256]{1,0:T(8,128)(2,1)S(1)}, bf16[400,256]{1,0:T(8,128)(2,1)S(1)}, u32[]{:S(2)}, u32[]{:S(2)}) %collective-permute-start.9) | collective-permute-done | bytes 204832 | tf_op jit(solution)/shard_map/ppermute | solution.py:471
  46.0 0.0 collective-permute-done.10.refs_3_
  46.0 0.4 place.1
  46.3 4.4 %collective-permute-start.11 = (bf16[384,256]{1,0:T(8,128)(2,1)S(1)}, bf16[384,256]{1,0:T(8,128)(2,1)S(1)}, u32[]{:S(2)}, u32[]{:S(2)}) collective-permute-start(bf16[384,256]{1,0:T(8,128)(2,1)S(1)} %get-tuple-element.42), channel_id=1, source_target_pairs={{1,0},{2,1},{3,2},{4,3},{5,4},{6,5},{7,6},{9,8},{10,9},{11,10},{12... | collective-permute-start | bytes 589832 | tf_op jit(solution)/shard_map/ppermute | solution.py:481
  50.7 4.1 %collective-permute-done.11 = bf16[384,256]{1,0:T(8,128)(2,1)S(1)} collective-permute-done((bf16[384,256]{1,0:T(8,128)(2,1)S(1)}, bf16[384,256]{1,0:T(8,128)(2,1)S(1)}, u32[]{:S(2)}, u32[]{:S(2)}) %collective-permute-start.11) | collective-permute-done | bytes 196640 | tf_op jit(solution)/shard_map/ppermute | solution.py:481
  54.8 0.8 %convert_add_fusion = f32[384,256]{1,0:T(8,128)} fusion(f32[384,256]{1,0:T(8,128)S(1)} %get-tuple-element.41, bf16[384,256]{1,0:T(8,128)(2,1)S(1)} %collective-permute-done.11), kind=kLoop, calls=%fused_computation | loop fusion | flops 196608 | bytes 983040 | tf_op jit(solution)/shard_map/add | solution.py:482
  (4 shorter events, 0.0 us)
Async XLA Ops:
  0.0 10.8 %collective-permute-start.2 = (bf16[384,256]{1,0:T(8,128)(2,1)}, bf16[384,256]{1,0:T(8,128)(2,1)S(1)}, u32[]{:S(2)}, u32[]{:S(2)}) collective-permute-start(bf16[384,256]{1,0:T(8,128)(2,1)} %bitcast.8), channel_id=1, source_target_pairs={{0,1},{1,2},{2,3},{3,4},{4,5},{5,6},{6,7},{8,9},{9,10},{10,11},{11... | collective-permute-start | bytes 589832 | tf_op jit(solution)/shard_map/ppermute | solution.py:360
  6.0 11.1 %collective-permute-start = (bf16[960,256]{1,0:T(8,128)(2,1)S(1)}, bf16[960,256]{1,0:T(8,128)(2,1)S(1)}, u32[]{:S(2)}, u32[]{:S(2)}) collective-permute-start(bf16[960,256]{1,0:T(8,128)(2,1)S(1)} %get-tuple-element.24), channel_id=1, source_target_pairs={{24,0},{16,8},{9,17},{1,25},{26,2},{18,10},{11,19},{3,27},{28,4},{... | collective-permute-start | bytes 1474568 | tf_op jit(solution)/shard_map/ppermute | solution.py:385
  12.0 16.1 %collective-permute-start.4 = (bf16[1760,256]{1,0:T(8,128)(2,1)S(1)}, bf16[1760,256]{1,0:T(8,128)(2,1)S(1)}, u32[]{:S(2)}, u32[]{:S(2)}) collective-permute-start(bf16[1760,256]{1,0:T(8,128)(2,1)S(1)} %get-tuple-element.28.refs_0_), channel_id=1, source_target_pairs={{16,0},{24,8},{1,17},{9,25},{18,2},{26,10},{3,19},{11,27},{20,4},{... | collective-permute-start | bytes 2703368 | tf_op jit(solution)/shard_map/ppermute | solution.py:404
  13.3 8.2 %collective-permute-start.5 = (bf16[400,256]{1,0:T(8,128)(2,1)S(1)}, bf16[400,256]{1,0:T(8,128)(2,1)S(1)}, u32[]{:S(2)}, u32[]{:S(2)}) collective-permute-start(bf16[400,256]{1,0:T(8,128)(2,1)S(1)} %get-tuple-element.31), channel_id=1, source_target_pairs={{24,0},{16,8},{9,17},{1,25},{26,2},{18,10},{11,19},{3,27},{28,4},{... | collective-permute-start | bytes 614408 | tf_op jit(solution)/shard_map/ppermute | solution.py:406
  14.6 13.4 %collective-permute-start.3 = (bf16[1680,256]{1,0:T(8,128)(2,1)S(1)}, bf16[1680,256]{1,0:T(8,128)(2,1)S(1)}, u32[]{:S(2)}, u32[]{:S(2)}) collective-permute-start(bf16[1680,256]{1,0:T(8,128)(2,1)S(1)} %get-tuple-element.29), channel_id=1, source_target_pairs={{8,0},{0,8},{25,17},{17,25},{10,2},{2,10},{27,19},{19,27},{12,4},{... | collective-permute-start | bytes 2580488 | tf_op jit(solution)/shard_map/ppermute | solution.py:403
  17.1 10.1 %collective-permute-start.1 = (bf16[960,256]{1,0:T(8,128)(2,1)S(1)}, bf16[960,256]{1,0:T(8,128)(2,1)S(1)}, u32[]{:S(2)}, u32[]{:S(2)}) collective-permute-start(bf16[960,256]{1,0:T(8,128)(2,1)S(1)} %collective-permute-done.first_ref), channel_id=1, source_target_pairs={{0,2},{8,10},{17,19},{25,27},{2,0},{10,8},{19,17},{27,25},{4,6},{1... | collective-permute-start | bytes 1474568 | tf_op jit(solution)/shard_map/ppermute | solution.py:407
  21.5 5.7 %copy-start.1 = (s32[2]{0:T(128)S(1)}, s32[2]{0:T(128)}, u32[]{:S(2)}) copy-start(s32[2]{0:T(128)} %anchors_hbm.1) | copy-start | bytes 28
  21.5 6.5 %copy-start = (bf16[2,2,128,256]{3,2,1,0:T(8,128)(2,1)S(1)}, bf16[2,2,128,256]{3,2,1,0:T(8,128)(2,1)}, u32[]{:S(2)}) copy-start(bf16[2,2,128,256]{3,2,1,0:T(8,128)(2,1)} %param.6) | copy-start | bytes 786436
  21.5 9.6 %collective-permute-start.7 = (bf16[640,256]{1,0:T(8,128)(2,1)S(1)}, bf16[640,256]{1,0:T(8,128)(2,1)S(1)}, u32[]{:S(2)}, u32[]{:S(2)}) collective-permute-start(bf16[640,256]{1,0:T(8,128)(2,1)S(1)} %hold.1.refs_3_), channel_id=1, source_target_pairs={{16,0},{24,8},{1,17},{9,25},{18,2},{26,10},{3,19},{11,27},{20,4},{... | collective-permute-start | bytes 983048 | tf_op jit(solution)/shard_map/ppermute | solution.py:418
  26.0 5.3 %collective-permute-start.6 = (bf16[640,256]{1,0:T(8,128)(2,1)S(1)}, bf16[640,256]{1,0:T(8,128)(2,1)S(1)}, u32[]{:S(2)}, u32[]{:S(2)}) collective-permute-start(bf16[640,256]{1,0:T(8,128)(2,1)S(1)} %hold.1.refs_3_), channel_id=1, source_target_pairs={{9,0},{1,8},{24,17},{16,25},{11,2},{3,10},{26,19},{18,27},{13,4},{... | collective-permute-start | bytes 983048 | tf_op jit(solution)/shard_map/ppermute | solution.py:418
  31.3 14.7 %collective-permute-start.10 = (bf16[416,256]{1,0:T(8,128)(2,1)S(1)}, bf16[416,256]{1,0:T(8,128)(2,1)S(1)}, u32[]{:S(2)}, u32[]{:S(2)}) collective-permute-start(bf16[416,256]{1,0:T(8,128)(2,1)S(1)} %get-tuple-element.40), channel_id=1, source_target_pairs={{0,24},{8,16},{17,9},{25,1},{2,26},{10,18},{19,11},{27,3},{4,28},{... | collective-permute-start | bytes 638984 | tf_op jit(solution)/shard_map/ppermute | solution.py:471
  32.6 13.4 %collective-permute-start.9 = (bf16[400,256]{1,0:T(8,128)(2,1)S(1)}, bf16[400,256]{1,0:T(8,128)(2,1)S(1)}, u32[]{:S(2)}, u32[]{:S(2)}) collective-permute-start(bf16[400,256]{1,0:T(8,128)(2,1)S(1)} %get-tuple-element.39), channel_id=1, source_target_pairs={{0,16},{8,24},{17,1},{25,9},{2,18},{10,26},{19,3},{27,11},{4,20},{... | collective-permute-start | bytes 614408 | tf_op jit(solution)/shard_map/ppermute | solution.py:471
  33.9 0.7 %collective-permute-start.8 = (bf16[384,256]{1,0:T(8,128)(2,1)S(1)}, bf16[384,256]{1,0:T(8,128)(2,1)S(1)}, u32[]{:S(2)}, u32[]{:S(2)}) collective-permute-start(bf16[384,256]{1,0:T(8,128)(2,1)S(1)} %get-tuple-element.38), channel_id=1, source_target_pairs={{0,8},{8,0},{17,25},{25,17},{2,10},{10,2},{19,27},{27,19},{4,12},{... | collective-permute-start | bytes 589832 | tf_op jit(solution)/shard_map/ppermute | solution.py:471
  46.3 8.5 %collective-permute-start.11 = (bf16[384,256]{1,0:T(8,128)(2,1)S(1)}, bf16[384,256]{1,0:T(8,128)(2,1)S(1)}, u32[]{:S(2)}, u32[]{:S(2)}) collective-permute-start(bf16[384,256]{1,0:T(8,128)(2,1)S(1)} %get-tuple-element.42), channel_id=1, source_target_pairs={{1,0},{2,1},{3,2},{4,3},{5,4},{6,5},{7,6},{9,8},{10,9},{11,10},{12... | collective-permute-start | bytes 589832 | tf_op jit(solution)/shard_map/ppermute | solution.py:481

commit v2 on v1

--- a/solution.py
+++ b/solution.py
@@ -361,7 +361,7 @@
     part = columns + rows // 2
     half_rows, win_rows = slots * part, slots * rows + TAIL
     early_rows = 2 * (half_rows - part) + win_rows
-    even = pltpu.VMEM((early_rows + 5 * TAIL, columns), bf16)
+    even = pltpu.VMEM((early_rows + 2 * TAIL, columns), bf16)
     odd = pltpu.VMEM((early_rows, columns), bf16)
     even_early, odd_early, late, far_half = pl.pallas_call(
         functools.partial(pack_kernel, group, sizes),
@@ -412,7 +412,7 @@
         out_specs=anywhere,
         input_output_aliases={0: 0},
         compiler_params=params(2),
-        cost_estimate=pl.CostEstimate(flops=36 * 10**8, bytes_accessed=0, transcendentals=0),
+        cost_estimate=pl.CostEstimate(flops=352 * 10**7, bytes_accessed=0, transcendentals=0),
         name="hold",
     )(late, far_window)
     lates = [lax.ppermute(late, BOTH, plan.ops_to_workers(r)) for r in (1, 2)]

time: 56 us -> 55.9 us (level)
  no operation moved by 1% of the time
where the time goes in v2:
time: 55.9 us; the launch traced here: 55.5 us
  starting transfers between devices  26.5 us (47%)
  waiting for transfers between devices  23.7 us (42%)
  Pallas kernels  3.76 us (7%)
  between operations  0.85 us (2%)
  other arithmetic  0.78 us (1%)
    ppermute x3, waiting for transfers between devices, on_device(): lax.ppermute(correlations[r], BOTH, plan.from_workers(r))  11 us
    ppermute x2, starting transfers between devices, on_device(): lates = [lax.ppermute(late, BOTH, plan.ops_to_workers(r)) for r in (1, 2)]  5.71 us
    ppermute x1, starting transfers between devices, on_device(): lax.ppermute(left, 'tile', [(i + 1, i) for i in range(plan.tiles - 1)])  4.77 us
    ppermute x1, starting transfers between devices, on_device(): lax.ppermute(tile_reflect, 'tile', [(i, i + 1) for i in range(plan.tiles...  4.58 us
    ppermute x1, starting transfers between devices, on_device(): far_half = lax.ppermute(far_half, BOTH, plan.to_workers(last))  4.1 us
    ppermute x1, waiting for transfers between devices, on_device(): lax.ppermute(left, 'tile', [(i + 1, i) for i in range(plan.tiles - 1)])  4.07 us
    ppermute x1, waiting for transfers between devices, on_device(): far_window = lax.ppermute(far_window, BOTH, plan.to_workers(last))  3.7 us
    ppermute x3, starting transfers between devices, on_device(): lax.ppermute(correlations[r], BOTH, plan.from_workers(r))  3.26 us
  transfers between devices with their start and end apart: 12, of which 6 were waited for; matrix products, arithmetic and copies ran while one was open for 0% of the time, Pallas kernels for 6%

profile of v2, /device:TPU:1, one launch (start us, length us, event | category | flops | bytes accessed | tf_op | source)
XLA Modules:
  0.0 55.5 jit_solution(6306473107607802351)
XLA Ops:
  0.0 4.6 %collective-permute-start.2 = (bf16[384,256]{1,0:T(8,128)(2,1)}, bf16[384,256]{1,0:T(8,128)(2,1)S(1)}, u32[]{:S(2)}, u32[]{:S(2)}) collective-permute-start(bf16[384,256]{1,0:T(8,128)(2,1)} %bitcast.8), channel_id=1, source_target_pairs={{0,1},{1,2},{2,3},{3,4},{4,5},{5,6},{6,7},{8,9},{9,10},{10,11},{11... | collective-permute-start | bytes 589832 | tf_op jit(solution)/shard_map/ppermute | solution.py:360
  4.6 1.4 %pack.1 = (bf16[1712,256]{1,0:T(8,128)(2,1)S(1)}, bf16[1680,256]{1,0:T(8,128)(2,1)S(1)}, bf16[640,256]{1,0:T(8,128)(2,1)S(1)}, bf16[960,256]{1,0:T(8,128)(2,1)S(1)}) custom-call(bf16[3,2,128,128]{3,2,1,0:T(8,128)(2,1)} %bitcast.7, bf16[3,2,256,256]{3,2,1,0:T(8,128)(2,1)} %bitcast.6), custom_call_target="tpu_custom_call" | custom-call | tf_op jit(solution)/shard_map/pack/pallas_call | solution.py:366
  6.0 4.1 %collective-permute-start = (bf16[960,256]{1,0:T(8,128)(2,1)S(1)}, bf16[960,256]{1,0:T(8,128)(2,1)S(1)}, u32[]{:S(2)}, u32[]{:S(2)}) collective-permute-start(bf16[960,256]{1,0:T(8,128)(2,1)S(1)} %get-tuple-element.24), channel_id=1, source_target_pairs={{24,0},{16,8},{9,17},{1,25},{26,2},{18,10},{11,19},{3,27},{28,4},{... | collective-permute-start | bytes 1474568 | tf_op jit(solution)/shard_map/ppermute | solution.py:385
  10.8 0.0 collective-permute-done.2.left_ref
  10.8 1.2 %windows.1 = (bf16[1712,256]{1,0:T(8,128)(2,1)S(1)}, bf16[1680,256]{1,0:T(8,128)(2,1)S(1)}, bf16[400,256]{1,0:T(8,128)(2,1)S(1)}) custom-call(s32[2]{0:T(128)} %anchors_hbm.1, s32[1]{0:T(128)S(6)} %copy.21.counts, bf16[384,256]{1,0:T(8,128)(2,1)S(1)} %collective-permute-done.2.left_ref, ...), custom_call_target="tpu_custom_call", output_to_operand_aliasing={{0}: (4, {}), {1}: (5, {})} | custom-call | flops 3000000000 | bytes 4194304 | tf_op jit(solution)/shard_map/windows/pallas_call | solution.py:386
  12.0 1.3 %collective-permute-start.4 = (bf16[1712,256]{1,0:T(8,128)(2,1)S(1)}, bf16[1712,256]{1,0:T(8,128)(2,1)S(1)}, u32[]{:S(2)}, u32[]{:S(2)}) collective-permute-start(bf16[1712,256]{1,0:T(8,128)(2,1)S(1)} %get-tuple-element.28.refs_0_), channel_id=1, source_target_pairs={{16,0},{24,8},{1,17},{9,25},{18,2},{26,10},{3,19},{11,27},{20,4},{... | collective-permute-start | bytes 2629640 | tf_op jit(solution)/shard_map/ppermute | solution.py:404
  13.3 1.3 %collective-permute-start.5 = (bf16[400,256]{1,0:T(8,128)(2,1)S(1)}, bf16[400,256]{1,0:T(8,128)(2,1)S(1)}, u32[]{:S(2)}, u32[]{:S(2)}) collective-permute-start(bf16[400,256]{1,0:T(8,128)(2,1)S(1)} %get-tuple-element.31), channel_id=1, source_target_pairs={{24,0},{16,8},{9,17},{1,25},{26,2},{18,10},{11,19},{3,27},{28,4},{... | collective-permute-start | bytes 614408 | tf_op jit(solution)/shard_map/ppermute | solution.py:406
  14.6 0.7 %collective-permute-start.3 = (bf16[1680,256]{1,0:T(8,128)(2,1)S(1)}, bf16[1680,256]{1,0:T(8,128)(2,1)S(1)}, u32[]{:S(2)}, u32[]{:S(2)}) collective-permute-start(bf16[1680,256]{1,0:T(8,128)(2,1)S(1)} %get-tuple-element.29), channel_id=1, source_target_pairs={{8,0},{0,8},{25,17},{17,25},{10,2},{2,10},{27,19},{19,27},{12,4},{... | collective-permute-start | bytes 2580488 | tf_op jit(solution)/shard_map/ppermute | solution.py:403
  15.4 1.8 %collective-permute-done.first_ref = bf16[960,256]{1,0:T(8,128)(2,1)S(1)} collective-permute-done((bf16[960,256]{1,0:T(8,128)(2,1)S(1)}, bf16[960,256]{1,0:T(8,128)(2,1)S(1)}, u32[]{:S(2)}, u32[]{:S(2)}) %collective-permute-start) | collective-permute-done | bytes 491552 | tf_op jit(solution)/shard_map/ppermute | solution.py:385
  17.1 0.7 %collective-permute-start.1 = (bf16[960,256]{1,0:T(8,128)(2,1)S(1)}, bf16[960,256]{1,0:T(8,128)(2,1)S(1)}, u32[]{:S(2)}, u32[]{:S(2)}) collective-permute-start(bf16[960,256]{1,0:T(8,128)(2,1)S(1)} %collective-permute-done.first_ref), channel_id=1, source_target_pairs={{0,2},{8,10},{17,19},{25,27},{2,0},{10,8},{19,17},{27,25},{4,6},{1... | collective-permute-start | bytes 1474568 | tf_op jit(solution)/shard_map/ppermute | solution.py:407
  17.8 3.7 %collective-permute-done.5.after_ref.refs_5_.refs_7_ = bf16[400,256]{1,0:T(8,128)(2,1)S(1)} collective-permute-done((bf16[400,256]{1,0:T(8,128)(2,1)S(1)}, bf16[400,256]{1,0:T(8,128)(2,1)S(1)}, u32[]{:S(2)}, u32[]{:S(2)}) %collective-permute-start.5) | collective-permute-done | bytes 204832 | tf_op jit(solution)/shard_map/ppermute | solution.py:406
  21.5 0.0 copy-start.1
  21.5 4.4 %collective-permute-start.7 = (bf16[640,256]{1,0:T(8,128)(2,1)S(1)}, bf16[640,256]{1,0:T(8,128)(2,1)S(1)}, u32[]{:S(2)}, u32[]{:S(2)}) collective-permute-start(bf16[640,256]{1,0:T(8,128)(2,1)S(1)} %hold.1.refs_3_), channel_id=1, source_target_pairs={{16,0},{24,8},{1,17},{9,25},{18,2},{26,10},{3,19},{11,27},{20,4},{... | collective-permute-start | bytes 983048 | tf_op jit(solution)/shard_map/ppermute | solution.py:418
  26.0 1.3 %collective-permute-start.6 = (bf16[640,256]{1,0:T(8,128)(2,1)S(1)}, bf16[640,256]{1,0:T(8,128)(2,1)S(1)}, u32[]{:S(2)}, u32[]{:S(2)}) collective-permute-start(bf16[640,256]{1,0:T(8,128)(2,1)S(1)} %hold.1.refs_3_), channel_id=1, source_target_pairs={{9,0},{1,8},{24,17},{16,25},{11,2},{3,10},{26,19},{18,27},{13,4},{... | collective-permute-start | bytes 983048 | tf_op jit(solution)/shard_map/ppermute | solution.py:418
  27.3 0.0 collective-permute-done.1.second_ref
  27.3 0.0 copy-done.1
  27.3 0.7 %join.1 = (bf16[1920,256]{1,0:T(8,128)(2,1)S(1)}, bf16[2,256,512]{2,1,0:T(8,128)(2,1)S(1)}) custom-call(s32[2]{0:T(128)S(1)} %copy-done.1, bf16[960,256]{1,0:T(8,128)(2,1)S(1)} %collective-permute-done.first_ref, bf16[960,256]{1,0:T(8,128)(2,1)S(1)} %collective-permute-done.1.second_ref), custom_call_target="tpu_custom_call" | custom-call | tf_op jit(solution)/shard_map/join/pallas_call | solution.py:419
  28.0 0.0 collective-permute-done.3.refs_1_
  28.0 0.0 collective-permute-done.4.refs_2_
  28.1 0.0 copy-done
  28.1 2.8 %collective-permute-done.7.refs_5_ = bf16[640,256]{1,0:T(8,128)(2,1)S(1)} collective-permute-done((bf16[640,256]{1,0:T(8,128)(2,1)S(1)}, bf16[640,256]{1,0:T(8,128)(2,1)S(1)}, u32[]{:S(2)}, u32[]{:S(2)}) %collective-permute-start.7) | collective-permute-done | bytes 327712 | tf_op jit(solution)/shard_map/ppermute | solution.py:418
  30.9 0.3 collective-permute-done.6.refs_4_
  31.3 1.3 %collective-permute-start.10 = (bf16[416,256]{1,0:T(8,128)(2,1)S(1)}, bf16[416,256]{1,0:T(8,128)(2,1)S(1)}, u32[]{:S(2)}, u32[]{:S(2)}) collective-permute-start(bf16[416,256]{1,0:T(8,128)(2,1)S(1)} %get-tuple-element.40), channel_id=1, source_target_pairs={{0,24},{8,16},{17,9},{25,1},{2,26},{10,18},{19,11},{27,3},{4,28},{... | collective-permute-start | bytes 638984 | tf_op jit(solution)/shard_map/ppermute | solution.py:471
  32.6 1.3 %collective-permute-start.9 = (bf16[400,256]{1,0:T(8,128)(2,1)S(1)}, bf16[400,256]{1,0:T(8,128)(2,1)S(1)}, u32[]{:S(2)}, u32[]{:S(2)}) collective-permute-start(bf16[400,256]{1,0:T(8,128)(2,1)S(1)} %get-tuple-element.39), channel_id=1, source_target_pairs={{0,16},{8,24},{17,1},{25,9},{2,18},{10,26},{19,3},{27,11},{4,20},{... | collective-permute-start | bytes 614408 | tf_op jit(solution)/shard_map/ppermute | solution.py:471
  33.9 0.7 %collective-permute-start.8 = (bf16[384,256]{1,0:T(8,128)(2,1)S(1)}, bf16[384,256]{1,0:T(8,128)(2,1)S(1)}, u32[]{:S(2)}, u32[]{:S(2)}) collective-permute-start(bf16[384,256]{1,0:T(8,128)(2,1)S(1)} %get-tuple-element.38), channel_id=1, source_target_pairs={{0,8},{8,0},{17,25},{25,17},{2,10},{10,2},{19,27},{27,19},{4,12},{... | collective-permute-start | bytes 589832 | tf_op jit(solution)/shard_map/ppermute | solution.py:471
  34.6 0.0 collective-permute-done.8.refs_1_
  34.6 11.0 %collective-permute-done.9.refs_2_ = bf16[400,256]{1,0:T(8,128)(2,1)S(1)} collective-permute-done((bf16[400,256]{1,0:T(8,128)(2,1)S(1)}, bf16[400,256]{1,0:T(8,128)(2,1)S(1)}, u32[]{:S(2)}, u32[]{:S(2)}) %collective-permute-start.9) | collective-permute-done | bytes 204832 | tf_op jit(solution)/shard_map/ppermute | solution.py:471
  45.5 0.0 collective-permute-done.10.refs_3_
  45.5 0.4 place.1
  45.9 4.8 %collective-permute-start.11 = (bf16[384,256]{1,0:T(8,128)(2,1)S(1)}, bf16[384,256]{1,0:T(8,128)(2,1)S(1)}, u32[]{:S(2)}, u32[]{:S(2)}) collective-permute-start(bf16[384,256]{1,0:T(8,128)(2,1)S(1)} %get-tuple-element.42), channel_id=1, source_target_pairs={{1,0},{2,1},{3,2},{4,3},{5,4},{6,5},{7,6},{9,8},{10,9},{11,10},{12... | collective-permute-start | bytes 589832 | tf_op jit(solution)/shard_map/ppermute | solution.py:481
  50.7 4.1 %collective-permute-done.11 = bf16[384,256]{1,0:T(8,128)(2,1)S(1)} collective-permute-done((bf16[384,256]{1,0:T(8,128)(2,1)S(1)}, bf16[384,256]{1,0:T(8,128)(2,1)S(1)}, u32[]{:S(2)}, u32[]{:S(2)}) %collective-permute-start.11) | collective-permute-done | bytes 196640 | tf_op jit(solution)/shard_map/ppermute | solution.py:481
  54.8 0.8 %convert_add_fusion = f32[384,256]{1,0:T(8,128)} fusion(f32[384,256]{1,0:T(8,128)S(1)} %get-tuple-element.41, bf16[384,256]{1,0:T(8,128)(2,1)S(1)} %collective-permute-done.11), kind=kLoop, calls=%fused_computation | loop fusion | flops 196608 | bytes 983040 | tf_op jit(solution)/shard_map/add | solution.py:482
  (4 shorter events, 0.0 us)
Async XLA Ops:
  0.0 10.8 %collective-permute-start.2 = (bf16[384,256]{1,0:T(8,128)(2,1)}, bf16[384,256]{1,0:T(8,128)(2,1)S(1)}, u32[]{:S(2)}, u32[]{:S(2)}) collective-permute-start(bf16[384,256]{1,0:T(8,128)(2,1)} %bitcast.8), channel_id=1, source_target_pairs={{0,1},{1,2},{2,3},{3,4},{4,5},{5,6},{6,7},{8,9},{9,10},{10,11},{11... | collective-permute-start | bytes 589832 | tf_op jit(solution)/shard_map/ppermute | solution.py:360
  6.0 11.1 %collective-permute-start = (bf16[960,256]{1,0:T(8,128)(2,1)S(1)}, bf16[960,256]{1,0:T(8,128)(2,1)S(1)}, u32[]{:S(2)}, u32[]{:S(2)}) collective-permute-start(bf16[960,256]{1,0:T(8,128)(2,1)S(1)} %get-tuple-element.24), channel_id=1, source_target_pairs={{24,0},{16,8},{9,17},{1,25},{26,2},{18,10},{11,19},{3,27},{28,4},{... | collective-permute-start | bytes 1474568 | tf_op jit(solution)/shard_map/ppermute | solution.py:385
  12.0 16.1 %collective-permute-start.4 = (bf16[1712,256]{1,0:T(8,128)(2,1)S(1)}, bf16[1712,256]{1,0:T(8,128)(2,1)S(1)}, u32[]{:S(2)}, u32[]{:S(2)}) collective-permute-start(bf16[1712,256]{1,0:T(8,128)(2,1)S(1)} %get-tuple-element.28.refs_0_), channel_id=1, source_target_pairs={{16,0},{24,8},{1,17},{9,25},{18,2},{26,10},{3,19},{11,27},{20,4},{... | collective-permute-start | bytes 2629640 | tf_op jit(solution)/shard_map/ppermute | solution.py:404
  13.3 8.2 %collective-permute-start.5 = (bf16[400,256]{1,0:T(8,128)(2,1)S(1)}, bf16[400,256]{1,0:T(8,128)(2,1)S(1)}, u32[]{:S(2)}, u32[]{:S(2)}) collective-permute-start(bf16[400,256]{1,0:T(8,128)(2,1)S(1)} %get-tuple-element.31), channel_id=1, source_target_pairs={{24,0},{16,8},{9,17},{1,25},{26,2},{18,10},{11,19},{3,27},{28,4},{... | collective-permute-start | bytes 614408 | tf_op jit(solution)/shard_map/ppermute | solution.py:406
  14.6 13.4 %collective-permute-start.3 = (bf16[1680,256]{1,0:T(8,128)(2,1)S(1)}, bf16[1680,256]{1,0:T(8,128)(2,1)S(1)}, u32[]{:S(2)}, u32[]{:S(2)}) collective-permute-start(bf16[1680,256]{1,0:T(8,128)(2,1)S(1)} %get-tuple-element.29), channel_id=1, source_target_pairs={{8,0},{0,8},{25,17},{17,25},{10,2},{2,10},{27,19},{19,27},{12,4},{... | collective-permute-start | bytes 2580488 | tf_op jit(solution)/shard_map/ppermute | solution.py:403
  17.1 10.1 %collective-permute-start.1 = (bf16[960,256]{1,0:T(8,128)(2,1)S(1)}, bf16[960,256]{1,0:T(8,128)(2,1)S(1)}, u32[]{:S(2)}, u32[]{:S(2)}) collective-permute-start(bf16[960,256]{1,0:T(8,128)(2,1)S(1)} %collective-permute-done.first_ref), channel_id=1, source_target_pairs={{0,2},{8,10},{17,19},{25,27},{2,0},{10,8},{19,17},{27,25},{4,6},{1... | collective-permute-start | bytes 1474568 | tf_op jit(solution)/shard_map/ppermute | solution.py:407
  21.5 5.7 %copy-start.1 = (s32[2]{0:T(128)S(1)}, s32[2]{0:T(128)}, u32[]{:S(2)}) copy-start(s32[2]{0:T(128)} %anchors_hbm.1) | copy-start | bytes 28
  21.5 6.5 %copy-start = (bf16[2,2,128,256]{3,2,1,0:T(8,128)(2,1)S(1)}, bf16[2,2,128,256]{3,2,1,0:T(8,128)(2,1)}, u32[]{:S(2)}) copy-start(bf16[2,2,128,256]{3,2,1,0:T(8,128)(2,1)} %param.6) | copy-start | bytes 786436
  21.5 9.4 %collective-permute-start.7 = (bf16[640,256]{1,0:T(8,128)(2,1)S(1)}, bf16[640,256]{1,0:T(8,128)(2,1)S(1)}, u32[]{:S(2)}, u32[]{:S(2)}) collective-permute-start(bf16[640,256]{1,0:T(8,128)(2,1)S(1)} %hold.1.refs_3_), channel_id=1, source_target_pairs={{16,0},{24,8},{1,17},{9,25},{18,2},{26,10},{3,19},{11,27},{20,4},{... | collective-permute-start | bytes 983048 | tf_op jit(solution)/shard_map/ppermute | solution.py:418
  26.0 5.3 %collective-permute-start.6 = (bf16[640,256]{1,0:T(8,128)(2,1)S(1)}, bf16[640,256]{1,0:T(8,128)(2,1)S(1)}, u32[]{:S(2)}, u32[]{:S(2)}) collective-permute-start(bf16[640,256]{1,0:T(8,128)(2,1)S(1)} %hold.1.refs_3_), channel_id=1, source_target_pairs={{9,0},{1,8},{24,17},{16,25},{11,2},{3,10},{26,19},{18,27},{13,4},{... | collective-permute-start | bytes 983048 | tf_op jit(solution)/shard_map/ppermute | solution.py:418
  31.3 14.3 %collective-permute-start.10 = (bf16[416,256]{1,0:T(8,128)(2,1)S(1)}, bf16[416,256]{1,0:T(8,128)(2,1)S(1)}, u32[]{:S(2)}, u32[]{:S(2)}) collective-permute-start(bf16[416,256]{1,0:T(8,128)(2,1)S(1)} %get-tuple-element.40), channel_id=1, source_target_pairs={{0,24},{8,16},{17,9},{25,1},{2,26},{10,18},{19,11},{27,3},{4,28},{... | collective-permute-start | bytes 638984 | tf_op jit(solution)/shard_map/ppermute | solution.py:471
  32.6 13.0 %collective-permute-start.9 = (bf16[400,256]{1,0:T(8,128)(2,1)S(1)}, bf16[400,256]{1,0:T(8,128)(2,1)S(1)}, u32[]{:S(2)}, u32[]{:S(2)}) collective-permute-start(bf16[400,256]{1,0:T(8,128)(2,1)S(1)} %get-tuple-element.39), channel_id=1, source_target_pairs={{0,16},{8,24},{17,1},{25,9},{2,18},{10,26},{19,3},{27,11},{4,20},{... | collective-permute-start | bytes 614408 | tf_op jit(solution)/shard_map/ppermute | solution.py:471
  33.9 0.7 %collective-permute-start.8 = (bf16[384,256]{1,0:T(8,128)(2,1)S(1)}, bf16[384,256]{1,0:T(8,128)(2,1)S(1)}, u32[]{:S(2)}, u32[]{:S(2)}) collective-permute-start(bf16[384,256]{1,0:T(8,128)(2,1)S(1)} %get-tuple-element.38), channel_id=1, source_target_pairs={{0,8},{8,0},{17,25},{25,17},{2,10},{10,2},{19,27},{27,19},{4,12},{... | collective-permute-start | bytes 589832 | tf_op jit(solution)/shard_map/ppermute | solution.py:471
  45.9 8.8 %collective-permute-start.11 = (bf16[384,256]{1,0:T(8,128)(2,1)S(1)}, bf16[384,256]{1,0:T(8,128)(2,1)S(1)}, u32[]{:S(2)}, u32[]{:S(2)}) collective-permute-start(bf16[384,256]{1,0:T(8,128)(2,1)S(1)} %get-tuple-element.42), channel_id=1, source_target_pairs={{1,0},{2,1},{3,2},{4,3},{5,4},{6,5},{7,6},{9,8},{10,9},{11,10},{12... | collective-permute-start | bytes 589832 | tf_op jit(solution)/shard_map/ppermute | solution.py:481

commit v3 on v2

--- a/solution.py
+++ b/solution.py
@@ -330,6 +330,19 @@
         placed = part if placed is None else placed + part
     left_out[...] = placed[:, :columns].astype(left_out.dtype)
     own_out[...] = placed[:, columns:]
+
+
+def sum_kernel(slots, own, other, out_hbm, held_sum, sem):
+    rows = own.shape[0] // slots
+    copies = []
+    for slot in range(slots):
+        lines = pl.ds(slot * rows, rows)
+        held_sum[lines, :] = own[lines, :] + other[lines, :].astype(jnp.float32)
+        copy = pltpu.make_async_copy(held_sum.at[lines, :], out_hbm.at[lines, :], sem.at[slot])
+        copy.start()
+        copies.append(copy)
+    for copy in copies:
+        copy.wait()
 
 
 def kept(array):
@@ -479,7 +492,15 @@
         name="place",
     )(held(shifts), *[held(part) for part in arrived])
     from_right = lax.ppermute(left, "tile", [(i + 1, i) for i in range(plan.tiles - 1)])
-    image = own + from_right.astype(jnp.float32)
+    image = pl.pallas_call(
+        functools.partial(sum_kernel, slots),
+        out_shape=jax.ShapeDtypeStruct(own.shape, jnp.float32),
+        in_specs=[vmem, vmem],
+        out_specs=anywhere,
+        scratch_shapes=[pltpu.VMEM(own.shape, jnp.float32), pltpu.SemaphoreType.DMA((slots,))],
+        compiler_params=params(8),
+        name="sum",
+    )(held(own), held(from_right))
     return image.reshape(1, slots, rows, columns)
 
 

time: 55.9 us -> 55.6 us (level)
  waiting for transfers between devices: 23.7 us -> 22.9 us
  Pallas kernels: 3.76 us -> 4.54 us
  other arithmetic: 0.78 us -> 0 us
    add x1 -> x0, other arithmetic: 0.78 us -> none  [on_device(): image = own + from_right.astype(jnp.float32)]
    pallas_call x0 -> x1, Pallas kernels: none -> 0.78 us  [on_device(): pl.pallas_call(functools.partial(sum_kernel, slots), out_shape=jax.ShapeD...]
where the time goes in v3:
time: 55.6 us; the launch traced here: 54.8 us
  starting transfers between devices  26.5 us (48%)
  waiting for transfers between devices  22.9 us (41%)
  Pallas kernels  4.54 us (8%)
  between operations  0.85 us (2%)
    ppermute x3, waiting for transfers between devices, on_device(): lax.ppermute(correlations[r], BOTH, plan.from_workers(r))  10.6 us
    ppermute x2, starting transfers between devices, on_device(): lates = [lax.ppermute(late, BOTH, plan.ops_to_workers(r)) for r in (1, 2)]  5.71 us
    ppermute x1, starting transfers between devices, on_device(): lax.ppermute(left, 'tile', [(i + 1, i) for i in range(plan.tiles - 1)])  4.77 us
    ppermute x1, starting transfers between devices, on_device(): lax.ppermute(tile_reflect, 'tile', [(i, i + 1) for i in range(plan.tiles...  4.58 us
    ppermute x1, starting transfers between devices, on_device(): far_half = lax.ppermute(far_half, BOTH, plan.to_workers(last))  4.1 us
    ppermute x1, waiting for transfers between devices, on_device(): far_window = lax.ppermute(far_window, BOTH, plan.to_workers(last))  3.7 us
    ppermute x1, waiting for transfers between devices, on_device(): lax.ppermute(left, 'tile', [(i + 1, i) for i in range(plan.tiles - 1)])  3.6 us
    ppermute x3, starting transfers between devices, on_device(): lax.ppermute(correlations[r], BOTH, plan.from_workers(r))  3.26 us
  transfers between devices with their start and end apart: 12, of which 6 were waited for; matrix products, arithmetic and copies ran while one was open for 0% of the time, Pallas kernels for 6%

profile of v3, /device:TPU:1, one launch (start us, length us, event | category | flops | bytes accessed | tf_op | source)
XLA Modules:
  0.0 54.8 jit_solution(5760655565985622529)
XLA Ops:
  0.0 4.6 %collective-permute-start.2 = (bf16[384,256]{1,0:T(8,128)(2,1)}, bf16[384,256]{1,0:T(8,128)(2,1)S(1)}, u32[]{:S(2)}, u32[]{:S(2)}) collective-permute-start(bf16[384,256]{1,0:T(8,128)(2,1)} %bitcast.8), channel_id=1, source_target_pairs={{0,1},{1,2},{2,3},{3,4},{4,5},{5,6},{6,7},{8,9},{9,10},{10,11},{11... | collective-permute-start | bytes 589832 | tf_op jit(solution)/shard_map/ppermute | solution.py:373
  4.6 1.4 %pack.1 = (bf16[1712,256]{1,0:T(8,128)(2,1)S(1)}, bf16[1680,256]{1,0:T(8,128)(2,1)S(1)}, bf16[640,256]{1,0:T(8,128)(2,1)S(1)}, bf16[960,256]{1,0:T(8,128)(2,1)S(1)}) custom-call(bf16[3,2,128,128]{3,2,1,0:T(8,128)(2,1)} %bitcast.7, bf16[3,2,256,256]{3,2,1,0:T(8,128)(2,1)} %bitcast.6), custom_call_target="tpu_custom_call" | custom-call | tf_op jit(solution)/shard_map/pack/pallas_call | solution.py:379
  6.0 4.1 %collective-permute-start = (bf16[960,256]{1,0:T(8,128)(2,1)S(1)}, bf16[960,256]{1,0:T(8,128)(2,1)S(1)}, u32[]{:S(2)}, u32[]{:S(2)}) collective-permute-start(bf16[960,256]{1,0:T(8,128)(2,1)S(1)} %get-tuple-element.24), channel_id=1, source_target_pairs={{24,0},{16,8},{9,17},{1,25},{26,2},{18,10},{11,19},{3,27},{28,4},{... | collective-permute-start | bytes 1474568 | tf_op jit(solution)/shard_map/ppermute | solution.py:398
  10.8 0.0 collective-permute-done.2.left_ref
  10.8 1.2 %windows.1 = (bf16[1712,256]{1,0:T(8,128)(2,1)S(1)}, bf16[1680,256]{1,0:T(8,128)(2,1)S(1)}, bf16[400,256]{1,0:T(8,128)(2,1)S(1)}) custom-call(s32[2]{0:T(128)} %anchors_hbm.1, s32[1]{0:T(128)S(6)} %copy.21.counts, bf16[384,256]{1,0:T(8,128)(2,1)S(1)} %collective-permute-done.2.left_ref, ...), custom_call_target="tpu_custom_call", output_to_operand_aliasing={{0}: (4, {}), {1}: (5, {})} | custom-call | flops 3000000000 | bytes 4194304 | tf_op jit(solution)/shard_map/windows/pallas_call | solution.py:399
  12.0 1.3 %collective-permute-start.4 = (bf16[1712,256]{1,0:T(8,128)(2,1)S(1)}, bf16[1712,256]{1,0:T(8,128)(2,1)S(1)}, u32[]{:S(2)}, u32[]{:S(2)}) collective-permute-start(bf16[1712,256]{1,0:T(8,128)(2,1)S(1)} %get-tuple-element.28.refs_0_), channel_id=1, source_target_pairs={{16,0},{24,8},{1,17},{9,25},{18,2},{26,10},{3,19},{11,27},{20,4},{... | collective-permute-start | bytes 2629640 | tf_op jit(solution)/shard_map/ppermute | solution.py:417
  13.3 1.3 %collective-permute-start.5 = (bf16[400,256]{1,0:T(8,128)(2,1)S(1)}, bf16[400,256]{1,0:T(8,128)(2,1)S(1)}, u32[]{:S(2)}, u32[]{:S(2)}) collective-permute-start(bf16[400,256]{1,0:T(8,128)(2,1)S(1)} %get-tuple-element.31), channel_id=1, source_target_pairs={{24,0},{16,8},{9,17},{1,25},{26,2},{18,10},{11,19},{3,27},{28,4},{... | collective-permute-start | bytes 614408 | tf_op jit(solution)/shard_map/ppermute | solution.py:419
  14.6 0.7 %collective-permute-start.3 = (bf16[1680,256]{1,0:T(8,128)(2,1)S(1)}, bf16[1680,256]{1,0:T(8,128)(2,1)S(1)}, u32[]{:S(2)}, u32[]{:S(2)}) collective-permute-start(bf16[1680,256]{1,0:T(8,128)(2,1)S(1)} %get-tuple-element.29), channel_id=1, source_target_pairs={{8,0},{0,8},{25,17},{17,25},{10,2},{2,10},{27,19},{19,27},{12,4},{... | collective-permute-start | bytes 2580488 | tf_op jit(solution)/shard_map/ppermute | solution.py:416
  15.4 1.8 %collective-permute-done.first_ref = bf16[960,256]{1,0:T(8,128)(2,1)S(1)} collective-permute-done((bf16[960,256]{1,0:T(8,128)(2,1)S(1)}, bf16[960,256]{1,0:T(8,128)(2,1)S(1)}, u32[]{:S(2)}, u32[]{:S(2)}) %collective-permute-start) | collective-permute-done | bytes 491552 | tf_op jit(solution)/shard_map/ppermute | solution.py:398
  17.1 0.7 %collective-permute-start.1 = (bf16[960,256]{1,0:T(8,128)(2,1)S(1)}, bf16[960,256]{1,0:T(8,128)(2,1)S(1)}, u32[]{:S(2)}, u32[]{:S(2)}) collective-permute-start(bf16[960,256]{1,0:T(8,128)(2,1)S(1)} %collective-permute-done.first_ref), channel_id=1, source_target_pairs={{0,2},{8,10},{17,19},{25,27},{2,0},{10,8},{19,17},{27,25},{4,6},{1... | collective-permute-start | bytes 1474568 | tf_op jit(solution)/shard_map/ppermute | solution.py:420
  17.8 3.7 %collective-permute-done.5.after_ref.refs_5_.refs_7_ = bf16[400,256]{1,0:T(8,128)(2,1)S(1)} collective-permute-done((bf16[400,256]{1,0:T(8,128)(2,1)S(1)}, bf16[400,256]{1,0:T(8,128)(2,1)S(1)}, u32[]{:S(2)}, u32[]{:S(2)}) %collective-permute-start.5) | collective-permute-done | bytes 204832 | tf_op jit(solution)/shard_map/ppermute | solution.py:419
  21.5 0.0 copy-start.1
  21.5 4.4 %collective-permute-start.7 = (bf16[640,256]{1,0:T(8,128)(2,1)S(1)}, bf16[640,256]{1,0:T(8,128)(2,1)S(1)}, u32[]{:S(2)}, u32[]{:S(2)}) collective-permute-start(bf16[640,256]{1,0:T(8,128)(2,1)S(1)} %hold.1.refs_3_), channel_id=1, source_target_pairs={{16,0},{24,8},{1,17},{9,25},{18,2},{26,10},{3,19},{11,27},{20,4},{... | collective-permute-start | bytes 983048 | tf_op jit(solution)/shard_map/ppermute | solution.py:431
  26.0 1.3 %collective-permute-start.6 = (bf16[640,256]{1,0:T(8,128)(2,1)S(1)}, bf16[640,256]{1,0:T(8,128)(2,1)S(1)}, u32[]{:S(2)}, u32[]{:S(2)}) collective-permute-start(bf16[640,256]{1,0:T(8,128)(2,1)S(1)} %hold.1.refs_3_), channel_id=1, source_target_pairs={{9,0},{1,8},{24,17},{16,25},{11,2},{3,10},{26,19},{18,27},{13,4},{... | collective-permute-start | bytes 983048 | tf_op jit(solution)/shard_map/ppermute | solution.py:431
  27.3 0.0 collective-permute-done.1.second_ref
  27.3 0.0 copy-done.1
  27.3 0.7 %join.1 = (bf16[1920,256]{1,0:T(8,128)(2,1)S(1)}, bf16[2,256,512]{2,1,0:T(8,128)(2,1)S(1)}) custom-call(s32[2]{0:T(128)S(1)} %copy-done.1, bf16[960,256]{1,0:T(8,128)(2,1)S(1)} %collective-permute-done.first_ref, bf16[960,256]{1,0:T(8,128)(2,1)S(1)} %collective-permute-done.1.second_ref), custom_call_target="tpu_custom_call" | custom-call | tf_op jit(solution)/shard_map/join/pallas_call | solution.py:432
  28.0 0.0 collective-permute-done.3.refs_1_
  28.0 0.0 collective-permute-done.4.refs_2_
  28.1 0.0 copy-done
  28.1 2.8 %collective-permute-done.7.refs_5_ = bf16[640,256]{1,0:T(8,128)(2,1)S(1)} collective-permute-done((bf16[640,256]{1,0:T(8,128)(2,1)S(1)}, bf16[640,256]{1,0:T(8,128)(2,1)S(1)}, u32[]{:S(2)}, u32[]{:S(2)}) %collective-permute-start.7) | collective-permute-done | bytes 327712 | tf_op jit(solution)/shard_map/ppermute | solution.py:431
  30.9 0.3 collective-permute-done.6.refs_4_
  31.3 1.3 %collective-permute-start.10 = (bf16[416,256]{1,0:T(8,128)(2,1)S(1)}, bf16[416,256]{1,0:T(8,128)(2,1)S(1)}, u32[]{:S(2)}, u32[]{:S(2)}) collective-permute-start(bf16[416,256]{1,0:T(8,128)(2,1)S(1)} %get-tuple-element.40), channel_id=1, source_target_pairs={{0,24},{8,16},{17,9},{25,1},{2,26},{10,18},{19,11},{27,3},{4,28},{... | collective-permute-start | bytes 638984 | tf_op jit(solution)/shard_map/ppermute | solution.py:484
  32.6 1.3 %collective-permute-start.9 = (bf16[400,256]{1,0:T(8,128)(2,1)S(1)}, bf16[400,256]{1,0:T(8,128)(2,1)S(1)}, u32[]{:S(2)}, u32[]{:S(2)}) collective-permute-start(bf16[400,256]{1,0:T(8,128)(2,1)S(1)} %get-tuple-element.39), channel_id=1, source_target_pairs={{0,16},{8,24},{17,1},{25,9},{2,18},{10,26},{19,3},{27,11},{4,20},{... | collective-permute-start | bytes 614408 | tf_op jit(solution)/shard_map/ppermute | solution.py:484
  33.9 0.7 %collective-permute-start.8 = (bf16[384,256]{1,0:T(8,128)(2,1)S(1)}, bf16[384,256]{1,0:T(8,128)(2,1)S(1)}, u32[]{:S(2)}, u32[]{:S(2)}) collective-permute-start(bf16[384,256]{1,0:T(8,128)(2,1)S(1)} %get-tuple-element.38), channel_id=1, source_target_pairs={{0,8},{8,0},{17,25},{25,17},{2,10},{10,2},{19,27},{27,19},{4,12},{... | collective-permute-start | bytes 589832 | tf_op jit(solution)/shard_map/ppermute | solution.py:484
  34.6 0.0 collective-permute-done.8.refs_1_
  34.6 10.6 %collective-permute-done.9.refs_2_ = bf16[400,256]{1,0:T(8,128)(2,1)S(1)} collective-permute-done((bf16[400,256]{1,0:T(8,128)(2,1)S(1)}, bf16[400,256]{1,0:T(8,128)(2,1)S(1)}, u32[]{:S(2)}, u32[]{:S(2)}) %collective-permute-start.9) | collective-permute-done | bytes 204832 | tf_op jit(solution)/shard_map/ppermute | solution.py:484
  45.2 0.0 collective-permute-done.10.refs_3_
  45.2 0.4 place.1
  45.6 4.8 %collective-permute-start.11 = (bf16[384,256]{1,0:T(8,128)(2,1)S(1)}, bf16[384,256]{1,0:T(8,128)(2,1)S(1)}, u32[]{:S(2)}, u32[]{:S(2)}) collective-permute-start(bf16[384,256]{1,0:T(8,128)(2,1)S(1)} %get-tuple-element.42), channel_id=1, source_target_pairs={{1,0},{2,1},{3,2},{4,3},{5,4},{6,5},{7,6},{9,8},{10,9},{11,10},{12... | collective-permute-start | bytes 589832 | tf_op jit(solution)/shard_map/ppermute | solution.py:494
  50.4 3.6 %collective-permute-done.11.other = bf16[384,256]{1,0:T(8,128)(2,1)S(1)} collective-permute-done((bf16[384,256]{1,0:T(8,128)(2,1)S(1)}, bf16[384,256]{1,0:T(8,128)(2,1)S(1)}, u32[]{:S(2)}, u32[]{:S(2)}) %collective-permute-start.11) | collective-permute-done | bytes 196640 | tf_op jit(solution)/shard_map/ppermute | solution.py:494
  54.0 0.8 %sum.1 = f32[384,256]{1,0:T(8,128)} custom-call(f32[384,256]{1,0:T(8,128)S(1)} %get-tuple-element.41.own, bf16[384,256]{1,0:T(8,128)(2,1)S(1)} %collective-permute-done.11.other), custom_call_target="tpu_custom_call" | custom-call | tf_op jit(solution)/shard_map/sum/pallas_call | solution.py:495
  (4 shorter events, 0.0 us)
Async XLA Ops:
  0.0 10.8 %collective-permute-start.2 = (bf16[384,256]{1,0:T(8,128)(2,1)}, bf16[384,256]{1,0:T(8,128)(2,1)S(1)}, u32[]{:S(2)}, u32[]{:S(2)}) collective-permute-start(bf16[384,256]{1,0:T(8,128)(2,1)} %bitcast.8), channel_id=1, source_target_pairs={{0,1},{1,2},{2,3},{3,4},{4,5},{5,6},{6,7},{8,9},{9,10},{10,11},{11... | collective-permute-start | bytes 589832 | tf_op jit(solution)/shard_map/ppermute | solution.py:373
  6.0 11.1 %collective-permute-start = (bf16[960,256]{1,0:T(8,128)(2,1)S(1)}, bf16[960,256]{1,0:T(8,128)(2,1)S(1)}, u32[]{:S(2)}, u32[]{:S(2)}) collective-permute-start(bf16[960,256]{1,0:T(8,128)(2,1)S(1)} %get-tuple-element.24), channel_id=1, source_target_pairs={{24,0},{16,8},{9,17},{1,25},{26,2},{18,10},{11,19},{3,27},{28,4},{... | collective-permute-start | bytes 1474568 | tf_op jit(solution)/shard_map/ppermute | solution.py:398
  12.0 16.1 %collective-permute-start.4 = (bf16[1712,256]{1,0:T(8,128)(2,1)S(1)}, bf16[1712,256]{1,0:T(8,128)(2,1)S(1)}, u32[]{:S(2)}, u32[]{:S(2)}) collective-permute-start(bf16[1712,256]{1,0:T(8,128)(2,1)S(1)} %get-tuple-element.28.refs_0_), channel_id=1, source_target_pairs={{16,0},{24,8},{1,17},{9,25},{18,2},{26,10},{3,19},{11,27},{20,4},{... | collective-permute-start | bytes 2629640 | tf_op jit(solution)/shard_map/ppermute | solution.py:417
  13.3 8.2 %collective-permute-start.5 = (bf16[400,256]{1,0:T(8,128)(2,1)S(1)}, bf16[400,256]{1,0:T(8,128)(2,1)S(1)}, u32[]{:S(2)}, u32[]{:S(2)}) collective-permute-start(bf16[400,256]{1,0:T(8,128)(2,1)S(1)} %get-tuple-element.31), channel_id=1, source_target_pairs={{24,0},{16,8},{9,17},{1,25},{26,2},{18,10},{11,19},{3,27},{28,4},{... | collective-permute-start | bytes 614408 | tf_op jit(solution)/shard_map/ppermute | solution.py:419
  14.6 13.4 %collective-permute-start.3 = (bf16[1680,256]{1,0:T(8,128)(2,1)S(1)}, bf16[1680,256]{1,0:T(8,128)(2,1)S(1)}, u32[]{:S(2)}, u32[]{:S(2)}) collective-permute-start(bf16[1680,256]{1,0:T(8,128)(2,1)S(1)} %get-tuple-element.29), channel_id=1, source_target_pairs={{8,0},{0,8},{25,17},{17,25},{10,2},{2,10},{27,19},{19,27},{12,4},{... | collective-permute-start | bytes 2580488 | tf_op jit(solution)/shard_map/ppermute | solution.py:416
  17.1 10.1 %collective-permute-start.1 = (bf16[960,256]{1,0:T(8,128)(2,1)S(1)}, bf16[960,256]{1,0:T(8,128)(2,1)S(1)}, u32[]{:S(2)}, u32[]{:S(2)}) collective-permute-start(bf16[960,256]{1,0:T(8,128)(2,1)S(1)} %collective-permute-done.first_ref), channel_id=1, source_target_pairs={{0,2},{8,10},{17,19},{25,27},{2,0},{10,8},{19,17},{27,25},{4,6},{1... | collective-permute-start | bytes 1474568 | tf_op jit(solution)/shard_map/ppermute | solution.py:420
  21.5 5.7 %copy-start.1 = (s32[2]{0:T(128)S(1)}, s32[2]{0:T(128)}, u32[]{:S(2)}) copy-start(s32[2]{0:T(128)} %anchors_hbm.1) | copy-start | bytes 28
  21.5 6.5 %copy-start = (bf16[2,2,128,256]{3,2,1,0:T(8,128)(2,1)S(1)}, bf16[2,2,128,256]{3,2,1,0:T(8,128)(2,1)}, u32[]{:S(2)}) copy-start(bf16[2,2,128,256]{3,2,1,0:T(8,128)(2,1)} %param.6) | copy-start | bytes 786436
  21.5 9.4 %collective-permute-start.7 = (bf16[640,256]{1,0:T(8,128)(2,1)S(1)}, bf16[640,256]{1,0:T(8,128)(2,1)S(1)}, u32[]{:S(2)}, u32[]{:S(2)}) collective-permute-start(bf16[640,256]{1,0:T(8,128)(2,1)S(1)} %hold.1.refs_3_), channel_id=1, source_target_pairs={{16,0},{24,8},{1,17},{9,25},{18,2},{26,10},{3,19},{11,27},{20,4},{... | collective-permute-start | bytes 983048 | tf_op jit(solution)/shard_map/ppermute | solution.py:431
  26.0 5.3 %collective-permute-start.6 = (bf16[640,256]{1,0:T(8,128)(2,1)S(1)}, bf16[640,256]{1,0:T(8,128)(2,1)S(1)}, u32[]{:S(2)}, u32[]{:S(2)}) collective-permute-start(bf16[640,256]{1,0:T(8,128)(2,1)S(1)} %hold.1.refs_3_), channel_id=1, source_target_pairs={{9,0},{1,8},{24,17},{16,25},{11,2},{3,10},{26,19},{18,27},{13,4},{... | collective-permute-start | bytes 983048 | tf_op jit(solution)/shard_map/ppermute | solution.py:431
  31.3 13.9 %collective-permute-start.10 = (bf16[416,256]{1,0:T(8,128)(2,1)S(1)}, bf16[416,256]{1,0:T(8,128)(2,1)S(1)}, u32[]{:S(2)}, u32[]{:S(2)}) collective-permute-start(bf16[416,256]{1,0:T(8,128)(2,1)S(1)} %get-tuple-element.40), channel_id=1, source_target_pairs={{0,24},{8,16},{17,9},{25,1},{2,26},{10,18},{19,11},{27,3},{4,28},{... | collective-permute-start | bytes 638984 | tf_op jit(solution)/shard_map/ppermute | solution.py:484
  32.6 12.6 %collective-permute-start.9 = (bf16[400,256]{1,0:T(8,128)(2,1)S(1)}, bf16[400,256]{1,0:T(8,128)(2,1)S(1)}, u32[]{:S(2)}, u32[]{:S(2)}) collective-permute-start(bf16[400,256]{1,0:T(8,128)(2,1)S(1)} %get-tuple-element.39), channel_id=1, source_target_pairs={{0,16},{8,24},{17,1},{25,9},{2,18},{10,26},{19,3},{27,11},{4,20},{... | collective-permute-start | bytes 614408 | tf_op jit(solution)/shard_map/ppermute | solution.py:484
  33.9 0.7 %collective-permute-start.8 = (bf16[384,256]{1,0:T(8,128)(2,1)S(1)}, bf16[384,256]{1,0:T(8,128)(2,1)S(1)}, u32[]{:S(2)}, u32[]{:S(2)}) collective-permute-start(bf16[384,256]{1,0:T(8,128)(2,1)S(1)} %get-tuple-element.38), channel_id=1, source_target_pairs={{0,8},{8,0},{17,25},{25,17},{2,10},{10,2},{19,27},{27,19},{4,12},{... | collective-permute-start | bytes 589832 | tf_op jit(solution)/shard_map/ppermute | solution.py:484
  45.6 8.4 %collective-permute-start.11 = (bf16[384,256]{1,0:T(8,128)(2,1)S(1)}, bf16[384,256]{1,0:T(8,128)(2,1)S(1)}, u32[]{:S(2)}, u32[]{:S(2)}) collective-permute-start(bf16[384,256]{1,0:T(8,128)(2,1)S(1)} %get-tuple-element.42), channel_id=1, source_target_pairs={{1,0},{2,1},{3,2},{4,3},{5,4},{6,5},{7,6},{9,8},{10,9},{11,10},{12... | collective-permute-start | bytes 589832 | tf_op jit(solution)/shard_map/ppermute | solution.py:494
